TPU v7x, 512 devices: a whole 4x8x8 slice. The times are simulated.
512 devices in a mesh: gx: 64 (over x, z, core), vert: 8 (over y).
Axes of the slice: x: 4, y: 8, z: 8, core: 2. Of those that a mesh axis runs over, the one named last changes fastest.
Arguments:
- prior_population: float32 [1024, 8, 32768], P('gx', None, 'vert'), may hold values from 0.1 to 2
- speeds: float32 [3, 32768], P(None, 'vert'), may hold values from 0.05 to 3
- jacobian: float32 [32768], P('vert'), may hold values from 0.5 to 1.5
- octant: int32 [256], P('vert'), may hold values from 0 to 7, as said below
- collision: float32 [1024, 8], P('gx'), may hold values from 1.953125e-05 to 0.6
- solid_mask: int32 [1024, 8], P('gx'), may hold values from 0 to 1, as said below
- wall_state: float32 [32768], P('vert'), may hold values from 0.1 to 2
- inflow: float32 [2, 8, 32768], P(None, None, 'vert'), may hold values from 0.1 to 2
Outputs:
- updated: float32 [1024, 8, 32768], P('gx', None, 'vert')
Inputs may be any that keep to these rules, and one draw needn't show every extreme that they name: Among the blocks of each aligned group of 4096 velocities, exactly half have an even octant. `solid_mask`: 1 marks the cells of one disc; the rows from 4 on meet it, the rows before never.
All inputs are finite; a program needn't handle non-finite values.
Results may differ from a plain program's by a relative error of at most 0.0003.
Values sent between devices are 32-bit elements; how exact they have to be, the bound alone decides.
A program may use at most 128 MiB of HBM per device.

v0:
```python
import math

import jax
import jax.numpy as jnp
from jax import lax
from jax.sharding import PartitionSpec as P

VEL = 32768
VBLK = 128
JAC = 4


VISCOUS_CONDUCT = 2.0 / 3.0
SOLID_DEPTH = 60.0
LOG_SPAN = 2.0 * math.log(60.0)
HIGHEST = lax.Precision.HIGHEST
TABLE_WIDTH = 128


def entering(value, axis, join, neutral, backward):
    count, mine = (lax.axis_size(axis), lax.axis_index(axis))
    pieces = jax.tree.map(lambda part: lax.all_gather(part, axis), value)
    if backward:
        pieces = jax.tree.map(lambda part: part[::-1], pieces)
        mine = count - 1 - mine
    running = jax.tree.map(
        lambda part, zero: jnp.full_like(part, 0) + jnp.asarray(zero, part.dtype), value, neutral
    )

    def lap(position, running):
        longer = join(running, jax.tree.map(lambda part: part[position], pieces))
        return jax.tree.map(lambda new, old: jnp.where(position < mine, new, old), longer, running)

    return lax.fori_loop(0, count - 1, lap, running)


def extended(value, sides, width):
    for axis, dim in sides:
        count, length = (lax.axis_size(axis), value.shape[dim])
        up = [(i, (i + 1) % count) for i in range(count - 1)]
        down = [(j, i) for i, j in up]
        last = lax.slice_in_dim(value, length - width, length, axis=dim)
        initial = lax.slice_in_dim(value, 0, width, axis=dim)
        before = lax.ppermute(last, axis, up)
        after = lax.ppermute(initial, axis, down)
        value = jnp.concatenate([before, value, after], axis=dim)
    return value


def velocity_set(speeds, jacobian, octant):
    octant_all = jnp.repeat(octant, VBLK)
    sign_first = (1 - 2 * (octant_all % 2)).astype(jnp.float32)
    sign_second = (1 - 2 * (octant_all // 2 % 2)).astype(jnp.float32)
    sign_third = (1 - 2 * (octant_all // 4)).astype(jnp.float32)
    weight = jacobian * speeds[0] * speeds[1] * speeds[2] * (LOG_SPAN**3 / VEL)
    return (sign_first * speeds[0], sign_second * speeds[1], sign_third * speeds[2], weight)


def moment_product(flat_rows, table):
    columns = table.shape[0]
    padded_table = jnp.pad(table, ((0, TABLE_WIDTH - columns), (0, 0)))
    product = jnp.dot(
        flat_rows, padded_table.T, precision=HIGHEST, preferred_element_type=jnp.float32
    )
    return product[:, :columns].T


def local_sweep(attenuation, deposit, backward):

    def advance(running, cell_terms):
        cum_decay = cell_terms[0] * running[0]
        cum_gain = cell_terms[0] * running[1] + cell_terms[1]
        return ((cum_decay, cum_gain), (cum_decay, cum_gain))

    initial = (
        jnp.ones(attenuation.shape[1:], jnp.float32),
        jnp.zeros(attenuation.shape[1:], jnp.float32),
    )
    return lax.scan(advance, initial, (attenuation, deposit), reverse=backward)


def paired_rows(field_pair):
    upper_edge_sites = jnp.pad(field_pair[:, :, 1:], ((0, 0), (0, 0), (0, 1)))
    lower_edge_sites = jnp.pad(field_pair[:, :, :-1], ((0, 0), (0, 0), (1, 0)))
    return upper_edge_sites + lower_edge_sites


def per_device(
    prior_population, speeds, jacobian, octant, collision, solid_mask, wall_state, inflow
):
    cell_count, row_count, local_vel = prior_population.shape
    velocity_x, velocity_y, velocity_z, weight = velocity_set(speeds, jacobian, octant)
    speed_sq = velocity_x * velocity_x + velocity_y * velocity_y + velocity_z * velocity_z
    flattened = prior_population.reshape(cell_count * row_count, local_vel)
    moment_table = jnp.stack(
        [
            weight,
            weight * velocity_x,
            weight * velocity_y,
            weight * velocity_z,
            0.5 * weight * speed_sq,
        ]
    )
    partial_sums = moment_product(flattened, moment_table).reshape(5, cell_count, row_count)
    summed = lax.psum(partial_sums, "vert")
    particle_concentration = summed[0]
    momentum = summed[1:4]
    kinetic_integral = summed[4]
    flow = momentum / particle_concentration
    bulk_motion_norm = flow[0] * flow[0] + flow[1] * flow[1] + flow[2] * flow[2]
    fluid_warmth = (2.0 * kinetic_integral / particle_concentration - bulk_motion_norm) / 3.0
    peculiar_x_part = velocity_x - flow[0][..., None]
    peculiar_y_part = velocity_y - flow[1][..., None]
    peculiar_z_part = velocity_z - flow[2][..., None]
    peculiar_norm = (
        peculiar_x_part * peculiar_x_part
        + peculiar_y_part * peculiar_y_part
        + peculiar_z_part * peculiar_z_part
    )
    gaussian_population = (particle_concentration * (2.0 * math.pi * fluid_warmth) ** (-1.5))[
        ..., None
    ] * jnp.exp(-peculiar_norm / (2.0 * fluid_warmth[..., None]))
    cubic = 0.5 * (prior_population * weight) * peculiar_norm
    local_heat = jnp.stack(
        [
            jnp.sum(cubic * peculiar_x_part, -1),
            jnp.sum(cubic * peculiar_y_part, -1),
            jnp.sum(cubic * peculiar_z_part, -1),
        ]
    )
    heat_vector = lax.psum(local_heat, "vert")
    skew_correction_multiplier = (
        peculiar_x_part * heat_vector[0][..., None]
        + peculiar_y_part * heat_vector[1][..., None]
        + peculiar_z_part * heat_vector[2][..., None]
    ) * (peculiar_norm / fluid_warmth[..., None] - 5.0)
    relaxed_goal_profile = gaussian_population * (
        1.0
        + (1.0 - VISCOUS_CONDUCT)
        * skew_correction_multiplier
        / (5.0 * particle_concentration * fluid_warmth * fluid_warmth)[..., None]
    )
    walled = solid_mask == 1
    source = jnp.where(walled[..., None], wall_state, relaxed_goal_profile)
    optical = jnp.where(walled, SOLID_DEPTH, collision)
    inverse = 1.0 / jnp.abs(velocity_x)
    attenuation = jnp.exp(-optical[..., None] * inverse)
    deposit = (1.0 - attenuation) * source
    blocks = octant.shape[0]
    block_order = jnp.argsort(octant % 2, stable=True)
    block_restore = jnp.argsort(block_order, stable=True)
    half_vel = local_vel // 2

    def arrange(values, permute):
        shaped = values.reshape(values.shape[:-1] + (blocks, VBLK))
        return jnp.take(shaped, permute, axis=-2).reshape(values.shape)

    attenuation_sorted = arrange(attenuation, block_order)
    deposit_sorted = arrange(deposit, block_order)
    inflow_sorted = arrange(inflow, block_order)

    def direction_sweep(attenuation_part, deposit_part, boundary, backward):
        composite, profile = local_sweep(attenuation_part, deposit_part, backward)

        def compose(earlier, later):
            return (later[0] * earlier[0], later[0] * earlier[1] + later[1])

        neutral = (
            jnp.ones(composite[0].shape, jnp.float32),
            jnp.zeros(composite[1].shape, jnp.float32),
        )
        if backward:
            preceding = entering((composite[0], composite[1]), "gx", compose, neutral, True)
        else:
            preceding = entering((composite[0], composite[1]), "gx", compose, neutral, False)
        incoming = preceding[0] * boundary + preceding[1]
        return profile[0] * incoming + profile[1]

    forward_part = direction_sweep(
        attenuation_sorted[..., :half_vel],
        deposit_sorted[..., :half_vel],
        inflow_sorted[0, :, :half_vel],
        False,
    )
    backward_part = direction_sweep(
        attenuation_sorted[..., half_vel:],
        deposit_sorted[..., half_vel:],
        inflow_sorted[1, :, half_vel:],
        True,
    )
    interim_split_portion = arrange(
        jnp.concatenate([forward_part, backward_part], -1), block_restore
    )
    half_table = jnp.stack([weight, 0.5 * weight * speed_sq])
    half_partial = moment_product(
        interim_split_portion.reshape(cell_count * row_count, local_vel), half_table
    ).reshape(2, cell_count, row_count)
    half_totals = lax.psum(half_partial, "vert")
    iterate_mismatch = jnp.stack(
        [half_totals[0] - particle_concentration, half_totals[1] - kinetic_integral]
    )
    row_index = jnp.arange(row_count)
    nearby_sites = (
        4.0
        - (row_index == 0).astype(jnp.float32)
        - (row_index == row_count - 1).astype(jnp.float32)
    )
    denominator_piece = 1.0 + nearby_sites * fluid_warmth
    acceleration_step = iterate_mismatch / denominator_piece
    for counter in range(JAC):
        padded_array = extended(acceleration_step, (("gx", 1),), 1)
        acceleration_step = (
            iterate_mismatch
            + fluid_warmth
            * (padded_array[:, 2:] + padded_array[:, :-2] + paired_rows(acceleration_step))
        ) / denominator_piece
    warmth_increment = (
        2.0 * acceleration_step[1] / 3.0
        - (fluid_warmth + bulk_motion_norm / 3.0) * acceleration_step[0]
    ) / particle_concentration
    mass_ratio = acceleration_step[0] / particle_concentration
    warmth_ratio = warmth_increment / fluid_warmth
    return interim_split_portion + gaussian_population * (
        mass_ratio[..., None]
        + warmth_ratio[..., None] * (peculiar_norm / (2.0 * fluid_warmth[..., None]) - 1.5)
    )


def solution(mesh):
    in_specs = (
        P("gx", None, "vert"),
        P(None, "vert"),
        P("vert"),
        P("vert"),
        P("gx", None),
        P("gx", None),
        P("vert"),
        P(None, None, "vert"),
    )
    out_specs = P("gx", None, "vert")
    return jax.shard_map(
        per_device, mesh=mesh, in_specs=in_specs, out_specs=out_specs, check_vma=False
    )
```

profile of v0, /device:TPU:2, one launch (start us, length us, event | category | flops | bytes accessed | tf_op | source)
XLA Modules:
  0.0 579.8 jit_solution(11056078307473045686)
XLA Ops:
  8.7 3.4 fusion.41
  12.3 30.4 %psum.21 = f32[5,16,8]{1,2,0:T(8,128)S(1)} all-reduce(f32[5,16,8]{1,2,0:T(8,128)S(1)} %copy.202), channel_id=1, replica_groups=mesh['gx'=64,'vert'=8] {'vert'}, use_global_device_ids=true, to_apply=%region_1.3 | all-reduce | flops 640 | bytes 5120 | tf_op jit(solution)/shard_map/psum | solution.py:105
  46.5 27.0 %psum.22 = f32[3,16,8]{1,2,0:T(8,128)S(1)} all-reduce(f32[3,16,8]{1,2,0:T(8,128)S(1)} %pad_maximum_fusion), channel_id=1, replica_groups=mesh['gx'=64,'vert'=8] {'vert'}, use_global_device_ids=true, to_apply=%region_5.7 | all-reduce | flops 384 | bytes 3072 | tf_op jit(solution)/shard_map/psum | solution.py:131
  74.4 3.5 fusion.18
  77.9 3.8 gather_fusion.1
  81.7 2.1 gather_fusion.2
  83.8 2.7 select_bitcast_fusion
  90.0 14.6 %while.72 = (s32[]{:T(128)}, f32[8,2048]{1,0:T(8,128)S(1)}, f32[8,2048]{1,0:T(8,128)S(1)}, f32[16,8,2048]{2,1,0:T(8,128)S(1)}, f32[16,8,2048]{2,1,0:T(8,128)S(1)...) while((s32[]{:T(128)}, f32[8,2048]{1,0:T(8,128)S(1)}, ...), condition=%wide.region_11.13_spmd.clone, body=%wide.region_10.12_spmd.clone.sunk | while | flops 81924 | bytes 524415 | solution.py:79
  106.3 15.1 %while.70 = (s32[]{:T(128)}, f32[8,2048]{1,0:T(8,128)S(1)}, f32[8,2048]{1,0:T(8,128)S(1)}, f32[16,8,2048]{2,1,0:T(8,128)S(1)}, f32[16,8,2048]{2,1,0:T(8,128)S(1)...) while((s32[]{:T(128)}, f32[8,2048]{1,0:T(8,128)S(1)}, ...), condition=%wide.region_7.9_spmd.clone, body=%wide.region_6.8_spmd.clone.sunk | while | flops 81923 | bytes 524395 | solution.py:79
  124.5 2.3 sort.32
  134.2 57.3 %all-gather.13.cloned.1.call-done = f32[512,2048]{1,0:T(8,128)} async-done(((f32[8,2048]{1,0:T(8,128)}), f32[512,2048]{1,0:T(8,128)}) %all-gather.13.cloned.1.call-update) | async-done | bytes 4194320 | tf_op jit(solution)/shard_map/all_gather | solution.py:22
  191.5 4.7 rev.6
  196.2 80.5 %all-gather.15.cloned.1.call-done = f32[512,2048]{1,0:T(8,128)} async-done(((f32[8,2048]{1,0:T(8,128)}), f32[512,2048]{1,0:T(8,128)}) %all-gather.15.cloned.1.call-update) | async-done | bytes 4194320 | tf_op jit(solution)/shard_map/all_gather | solution.py:22
  276.7 4.7 rev.7
  281.4 59.3 %while.73 = (s32[]{:T(128)}, f32[8,2048]{1,0:T(8,128)S(1)}, f32[8,2048]{1,0:T(8,128)S(1)}, s32[]{:T(128)}, f32[64,8,2048]{2,1,0:T(8,128)}, /*index=5*/f32[64,8,2048]{2,1,0:T(8,128)}, s32[]{:T(128)}, s32[]{:T(128)}) while((s32[]{:T(128)}, f32[8,2048]{1,0:T(8,128)S(1)}, f32[8,2048]{1,0:T(8,128)S(1)}, s32[]{:T(128)}, ...), condition=%wide.region_13.15_spmd.clone, body=%wide.region_12.14_spmd.clone.sunk | while | flops 114692 | bytes 393325 | solution.py:34
  340.7 21.2 %all-gather.9.cloned.1.call-done = f32[512,2048]{1,0:T(8,128)} async-done(((f32[8,2048]{1,0:T(8,128)}), f32[512,2048]{1,0:T(8,128)}) %all-gather.9.cloned.1.call-update) | async-done | bytes 4194320 | tf_op jit(solution)/shard_map/all_gather | solution.py:22
  361.9 85.0 %all-gather.11.cloned.1.call-done = f32[512,2048]{1,0:T(8,128)} async-done(((f32[8,2048]{1,0:T(8,128)}), f32[512,2048]{1,0:T(8,128)}) %all-gather.11.cloned.1.call-update) | async-done | bytes 4194320 | tf_op jit(solution)/shard_map/all_gather | solution.py:22
  447.0 59.3 %while.71 = (s32[]{:T(128)}, f32[8,2048]{1,0:T(8,128)S(1)}, f32[8,2048]{1,0:T(8,128)S(1)}, s32[]{:T(128)}, f32[64,8,2048]{2,1,0:T(8,128)}, /*index=5*/f32[64,8,2048]{2,1,0:T(8,128)}, s32[]{:T(128)}, s32[]{:T(128)}) while((s32[]{:T(128)}, f32[8,2048]{1,0:T(8,128)S(1)}, f32[8,2048]{1,0:T(8,128)S(1)}, s32[]{:T(128)}, ...), condition=%wide.region_9.11_spmd.clone, body=%wide.region_8.10_spmd.clone.sunk | while | flops 114692 | bytes 393325 | solution.py:34
  507.8 2.3 gather_fusion.3
  510.1 1.9 select_bitcast_fusion.3
  513.4 2.7 fusion.46
  516.3 17.2 %psum.23 = f32[2,16,8]{1,2,0:T(8,128)S(1)} all-reduce(f32[2,16,8]{1,2,0:T(8,128)S(1)} %copy.225), channel_id=1, replica_groups=mesh['gx'=64,'vert'=8] {'vert'}, use_global_device_ids=true, to_apply=%region_15.17 | all-reduce | flops 256 | bytes 2048 | tf_op jit(solution)/shard_map/psum | solution.py:198
  535.6 2.4 collective-permute-start.1
  538.0 4.7 collective-permute-done.1
  542.8 1.9 collective-permute-start.2
  544.8 2.4 collective-permute-start.3
  547.2 4.7 collective-permute-done.3
  553.9 2.4 collective-permute-start.5
  556.4 4.7 collective-permute-done.5
  563.1 2.4 collective-permute-start.7
  565.5 4.7 collective-permute-done.7
  570.5 2.8 fusion.30
  (344 shorter events, 176.7 us)
Async XLA Ops:
  6.5 123.3 %copy-start = (f32[2,8,4096]{2,1,0:T(8,128)S(1)}, f32[2,8,4096]{2,1,0:T(8,128)}, u32[]{:S(2)}) copy-start(f32[2,8,4096]{2,1,0:T(8,128)} %param.25) | copy-start | bytes 786436
  6.5 36.2 %copy-start.37 = (s32[32]{0:T(128)S(1)}, s32[32]{0:T(128)}, u32[]{:S(2)}) copy-start(s32[32]{0:T(128)} %param.21) | copy-start | bytes 388
  6.5 38.1 %copy-start.2 = (f32[16,8,4096]{2,1,0:T(8,128)S(1)}, f32[16,8,4096]{2,1,0:T(8,128)}, u32[]{:S(2)}) copy-start(f32[16,8,4096]{2,1,0:T(8,128)} %param.18) | copy-start | bytes 6291460
  6.5 185.0 %all-gather.13.cloned.1.call-start = ((), (), s32[]{:S(2)}) async-start(), calls=%async_computation.2 | async-start | bytes 4259840 | tf_op jit(solution)/shard_map/all_gather | solution.py:22
  8.5 37.8 %copy-start.11 = (f32[4096]{0:T(1024)}, f32[4096]{0:T(1024)S(1)}, u32[]{:S(2)}) copy-start(f32[4096]{0:T(1024)S(1)} %get-tuple-element.584) | copy-start | bytes 49156
  8.5 37.8 %copy-start.13 = (f32[4096]{0:T(1024)}, f32[4096]{0:T(1024)S(1)}, u32[]{:S(2)}) copy-start(f32[4096]{0:T(1024)S(1)} %get-tuple-element.585) | copy-start | bytes 49156
  8.5 37.8 %copy-start.15 = (f32[4096]{0:T(1024)}, f32[4096]{0:T(1024)S(1)}, u32[]{:S(2)}) copy-start(f32[4096]{0:T(1024)S(1)} %get-tuple-element.586) | copy-start | bytes 49156
  8.5 37.8 %copy-start.21 = (f32[4096]{0:T(1024)}, f32[4096]{0:T(1024)S(1)}, u32[]{:S(2)}) copy-start(f32[4096]{0:T(1024)S(1)} %get-tuple-element.583) | copy-start | bytes 49156
  8.6 37.8 %copy-start.17 = (f32[4096]{0:T(1024)}, f32[4096]{0:T(1024)S(1)}, u32[]{:S(2)}) copy-start(f32[4096]{0:T(1024)S(1)} %get-tuple-element.622) | copy-start | bytes 49156
  8.7 65.4 %copy-start.35 = (f32[16,8]{0,1:T(8,128)S(1)}, f32[16,8]{0,1:T(8,128)}, u32[]{:S(2)}) copy-start(f32[16,8]{0,1:T(8,128)} %param.22) | copy-start | bytes 1540
  8.7 65.4 %copy-start.36 = (s32[16,8]{0,1:T(8,128)S(1)}, s32[16,8]{0,1:T(8,128)}, u32[]{:S(2)}) copy-start(s32[16,8]{0,1:T(8,128)} %param.23) | copy-start | bytes 1540
  8.7 65.7 %copy-start.33 = (f32[4096]{0:T(1024)S(1)}, f32[4096]{0:T(1024)}, u32[]{:S(2)}) copy-start(f32[4096]{0:T(1024)} %param.24) | copy-start | bytes 49156
  44.4 39.4 %copy-start.38 = (pred[32]{0:T(512)(128)(4,1)}, pred[32]{0:T(512)(128)(4,1)S(1)}, u32[]{:S(2)}) copy-start(pred[32]{0:T(512)(128)(4,1)S(1)} %compare_and_fusion.1) | copy-start | bytes 100
  105.3 171.4 %all-gather.15.cloned.1.call-start = ((), (), s32[]{:S(2)}) async-start(), calls=%async_computation.3 | async-start | bytes 4259840 | tf_op jit(solution)/shard_map/all_gather | solution.py:22
  106.1 255.8 %all-gather.9.cloned.1.call-start = ((), (), s32[]{:S(2)}) async-start(), calls=%async_computation | async-start | bytes 4259840 | tf_op jit(solution)/shard_map/all_gather | solution.py:22
  122.1 324.9 %all-gather.11.cloned.1.call-start = ((), (), s32[]{:S(2)}) async-start(), calls=%async_computation.1 | async-start | bytes 4259840 | tf_op jit(solution)/shard_map/all_gather | solution.py:22
  513.3 57.1 %copy-start.12 = (f32[4096]{0:T(1024)S(1)}, f32[4096]{0:T(1024)}, u32[]{:S(2)}) copy-start(f32[4096]{0:T(1024)} %copy-done.11) | copy-start | bytes 49156
  513.3 57.1 %copy-start.14 = (f32[4096]{0:T(1024)S(1)}, f32[4096]{0:T(1024)}, u32[]{:S(2)}) copy-start(f32[4096]{0:T(1024)} %copy-done.13) | copy-start | bytes 49156
  513.3 57.1 %copy-start.16 = (f32[4096]{0:T(1024)S(1)}, f32[4096]{0:T(1024)}, u32[]{:S(2)}) copy-start(f32[4096]{0:T(1024)} %copy-done.15) | copy-start | bytes 49156
  513.3 57.1 %copy-start.24 = (f32[16,8]{1,0:T(8,128)S(1)}, f32[16,8]{1,0:T(8,128)}, u32[]{:S(2)}) copy-start(f32[16,8]{1,0:T(8,128)} %copy-done.23) | copy-start | bytes 1540
  513.3 57.1 %copy-start.26 = (f32[16,8]{1,0:T(8,128)S(1)}, f32[16,8]{1,0:T(8,128)}, u32[]{:S(2)}) copy-start(f32[16,8]{1,0:T(8,128)} %copy-done.25) | copy-start | bytes 1540
  513.3 57.1 %copy-start.28 = (f32[16,8]{1,0:T(8,128)S(1)}, f32[16,8]{1,0:T(8,128)}, u32[]{:S(2)}) copy-start(f32[16,8]{1,0:T(8,128)} %copy-done.27) | copy-start | bytes 1540
  513.3 57.1 %copy-start.30 = (f32[16,8]{1,0:T(8,128)S(1)}, f32[16,8]{1,0:T(8,128)}, u32[]{:S(2)}) copy-start(f32[16,8]{1,0:T(8,128)} %copy-done.29) | copy-start | bytes 1540
  513.3 57.1 %copy-start.32 = (f32[16,8]{1,0:T(8,128)S(1)}, f32[16,8]{1,0:T(8,128)}, u32[]{:S(2)}) copy-start(f32[16,8]{1,0:T(8,128)} %copy-done.31) | copy-start | bytes 1540
  533.7 4.3 collective-permute-start
  535.6 7.1 %collective-permute-start.1 = (f32[2,1,8]{1,2,0:T(8,128)S(1)}, f32[2,1,8]{1,2,0:T(8,128)S(1)}, u32[]{:S(2)}, u32[]{:S(2)}) collective-permute-start(f32[2,1,8]{1,2,0:T(8,128)S(1)} %get-tuple-element.644), channel_id=1, source_target_pairs={{0,8},{8,16},{16,24},{24,32},{32,40},{40,48},{48,56},{56,64},{64,7... | collective-permute-start | bytes 200 | tf_op jit(solution)/shard_map/ppermute | solution.py:44
  542.8 4.3 collective-permute-start.2
  544.8 7.1 %collective-permute-start.3 = (f32[2,1,8]{1,2,0:T(8,128)S(1)}, f32[2,1,8]{1,2,0:T(8,128)S(1)}, u32[]{:S(2)}, u32[]{:S(2)}) collective-permute-start(f32[2,1,8]{1,2,0:T(8,128)S(1)} %get-tuple-element.640), channel_id=1, source_target_pairs={{0,8},{8,16},{16,24},{24,32},{32,40},{40,48},{48,56},{56,64},{64,7... | collective-permute-start | bytes 200 | tf_op jit(solution)/shard_map/ppermute | solution.py:44
  552.0 4.3 collective-permute-start.4
  553.9 7.1 %collective-permute-start.5 = (f32[2,1,8]{1,2,0:T(8,128)S(1)}, f32[2,1,8]{1,2,0:T(8,128)S(1)}, u32[]{:S(2)}, u32[]{:S(2)}) collective-permute-start(f32[2,1,8]{1,2,0:T(8,128)S(1)} %get-tuple-element.636), channel_id=1, source_target_pairs={{0,8},{8,16},{16,24},{24,32},{32,40},{40,48},{48,56},{56,64},{64,7... | collective-permute-start | bytes 200 | tf_op jit(solution)/shard_map/ppermute | solution.py:44
  561.2 4.3 collective-permute-start.6
  563.1 7.1 %collective-permute-start.7 = (f32[2,1,8]{1,2,0:T(8,128)S(1)}, f32[2,1,8]{1,2,0:T(8,128)S(1)}, u32[]{:S(2)}, u32[]{:S(2)}) collective-permute-start(f32[2,1,8]{1,2,0:T(8,128)S(1)} %get-tuple-element.632), channel_id=1, source_target_pairs={{0,8},{8,16},{16,24},{24,32},{32,40},{40,48},{48,56},{56,64},{64,7... | collective-permute-start | bytes 200 | tf_op jit(solution)/shard_map/ppermute | solution.py:44
  (22 other events, 247.1 us)
Sparse Core Ops, SparseCore 0:
  105.4 86.0 all-gather.12
  194.9 81.7 all-gather.14
  280.1 81.7 all-gather.8
  365.1 81.7 all-gather.10
where the time goes:
time: 588 us; the launch traced here: 580 us
  waiting for transfers between devices  264 us (45%)
  other arithmetic  170 us (29%)
  blocking collectives  74.6 us (13%)
  local copies, waits for them, and re-layouts  30.2 us (5%)
  starting transfers between devices  17.6 us (3%)
  between operations  13.9 us (2%)
  matrix products  6.12 us (1%)
    all_gather x4, waiting for transfers between devices, entering(): pieces = jax.tree.map(lambda part: lax.all_gather(part, axis), value)  244 us
    select_n x126, other arithmetic, lap(): jnp.where(position < mine, new, old)  116 us
    psum x1, blocking collectives, per_device(): summed = lax.psum(partial_sums, 'vert')  30.4 us
    dynamic_update_slice x32, other arithmetic, local_sweep(): return lax.scan(advance, initial, (attenuation, deposit), reverse=backward)  29.2 us
    psum x1, blocking collectives, per_device(): heat_vector = lax.psum(local_heat, 'vert')  27 us
    ppermute x4, waiting for transfers between devices, extended(): before = lax.ppermute(last, axis, up)  18.6 us
    psum x1, blocking collectives, per_device(): half_totals = lax.psum(half_partial, 'vert')  17.2 us
  transfers between devices with their start and end apart: 12, of which 8 were waited for; matrix products, arithmetic and copies ran while one was open for 16% of the time, Pallas kernels for 0%

commit v1 on v0

v1 whole, which is shorter than its diff:
```python
import functools
import math

import jax
import jax.numpy as jnp
from jax import lax
from jax.experimental import pallas as pl
from jax.experimental.pallas import tpu as pltpu
from jax.sharding import PartitionSpec as P

VEL = 32768
LANES = 128
JAC = 4
CHUNKS = 4
MOMENTS = 13
SOLID_DEPTH = 60.0
LOG_SPAN = 2.0 * math.log(60.0)
F32 = jnp.float32
MESH = pl.DeviceIdType.MESH

CX, CY, CZ, WEIGHT, WEIGHT_E, NEG_INV, WALL, BACKWARD = range(8)


def lane_block(index):
    return pl.ds(pl.multiple_of(index * LANES, LANES), LANES)


def table_row(base_ref, row, block, rows):
    return jnp.broadcast_to(base_ref[row : row + 1, lane_block(block)], (rows, LANES))


def lane_index(rows):
    return lax.broadcasted_iota(jnp.int32, (rows, LANES), 1)


def moments_kernel(base_ref, prior_ref, out_ref, table, totals):
    columns, rows, width = prior_ref.shape
    blocks = width // LANES
    step = pl.program_id(0)

    @pl.when(step == 0)
    def _():
        totals[...] = jnp.zeros_like(totals)

    for b in range(blocks):
        cx, cy, cz, w = (table_row(base_ref, row, b, rows) for row in (CX, CY, CZ, WEIGHT))
        square = cx * cx + cy * cy + cz * cz
        wx, wy, wz = w * cx, w * cy, w * cz
        entries = (
            w, wx, wy, wz,
            wx * cx, wx * cy, wx * cz, wy * cy, wy * cz, wz * cz,
            wx * square, wy * square, wz * square,
        )
        for m, entry in enumerate(entries):
            table[m, b] = entry

    def pair(g, carry):
        first = [totals[2 * g, m] for m in range(MOMENTS)]
        second = [totals[2 * g + 1, m] for m in range(MOMENTS)]
        for b in range(blocks):
            left = prior_ref[2 * g, :, b * LANES : (b + 1) * LANES]
            right = prior_ref[2 * g + 1, :, b * LANES : (b + 1) * LANES]
            for m in range(MOMENTS):
                entry = table[m, b]
                first[m] = first[m] + left * entry
                second[m] = second[m] + right * entry
        for m in range(MOMENTS):
            totals[2 * g, m] = first[m]
            totals[2 * g + 1, m] = second[m]
        return carry

    lax.fori_loop(0, columns // 2, pair, 0)

    @pl.when(step == pl.num_programs(0) - 1)
    def _():
        lane = lane_index(rows)

        def pack(i, packed):
            packed = list(packed)
            for m in range(MOMENTS):
                total = jnp.sum(totals[i, m], axis=1, keepdims=True)
                spot = lane == (m % 8) * 16 + i
                packed[m // 8] = jnp.where(spot, total, packed[m // 8])
            return tuple(packed)

        zero = jnp.zeros((rows, LANES), F32)
        low, high = lax.fori_loop(0, columns, pack, (zero, zero))
        out_ref[:, :LANES] = low
        out_ref[:, LANES:] = high


def vert_sum_kernel(count, mine_ref, out_ref, slots, send_sem, recv_sem):
    me = lax.axis_index("vert")
    barrier = pltpu.get_barrier_semaphore()
    for k in range(1, count):
        pl.semaphore_signal(
            barrier, inc=1, device_id={"vert": lax.rem(me + k, count)}, device_id_type=MESH
        )
    pl.semaphore_wait(barrier, count - 1)

    def copy_to(k):
        return pltpu.make_async_remote_copy(
            src_ref=mine_ref,
            dst_ref=slots.at[me],
            send_sem=send_sem.at[k],
            recv_sem=recv_sem.at[me],
            device_id={"vert": lax.rem(me + k, count)},
            device_id_type=MESH,
        )

    for k in range(1, count):
        copy_to(k).start()
    slots[me] = mine_ref[...]
    for k in range(1, count):
        other = lax.rem(me + k, count)
        pltpu.make_async_remote_copy(
            src_ref=mine_ref,
            dst_ref=slots.at[other],
            send_sem=send_sem.at[k],
            recv_sem=recv_sem.at[other],
            device_id={"vert": other},
            device_id_type=MESH,
        ).wait_recv()
    total = slots[0]
    for k in range(1, count):
        total = total + slots[k]
    out_ref[...] = total
    for k in range(1, count):
        copy_to(k).wait_send()


def cell_values(sums_ref):
    low, high = sums_ref[:, :LANES], sums_ref[:, LANES:]
    picked = []
    for m in range(MOMENTS):
        source = low if m < 8 else high
        shift = (LANES - 16 * (m % 8)) % LANES
        picked.append(pltpu.roll(source, shift, 1) if shift else source)
    valid = lane_index(low.shape[0]) < 16
    rho = jnp.where(valid, picked[0], 1.0)
    sx, sy, sz, pxx, pxy, pxz, pyy, pyz, pzz, qx, qy, qz = (
        jnp.where(valid, value, 1.0) for value in picked[1:]
    )
    ux, uy, uz = sx / rho, sy / rho, sz / rho
    flow_sq = ux * ux + uy * uy + uz * uz
    second = pxx + pyy + pzz
    warmth = (second / rho - flow_sq) / 3.0
    swirl = rho * flow_sq
    heat_x = 0.5 * (qx - second * ux) - (ux * pxx + uy * pxy + uz * pxz) + swirl * ux
    heat_y = 0.5 * (qy - second * uy) - (ux * pxy + uy * pyy + uz * pyz) + swirl * uy
    heat_z = 0.5 * (qz - second * uz) - (ux * pxz + uy * pyz + uz * pzz) + swirl * uz
    return {
        "rho": rho, "ux": ux, "uy": uy, "uz": uz, "flow_sq": flow_sq, "warmth": warmth,
        "energy": 0.5 * second, "hx": heat_x, "hy": heat_y, "hz": heat_z,
    }


def maxwell_scale(cell):
    warmth = cell["warmth"]
    area = (2.0 * math.pi) * warmth
    return cell["rho"] / (area * jnp.sqrt(area))


def spread(value, column, rows):
    return jnp.broadcast_to(value[:, column : column + 1], (rows, LANES))


def sweep_kernel(octant_ref, sums_ref, base_ref, cell_ref, gain_ref, message_ref, coef):
    columns, rows, width = gain_ref.shape
    blocks = width // LANES
    step = pl.program_id(0)

    @pl.when(step == 0)
    def _():
        cell = cell_values(sums_ref)
        warmth, rho = cell["warmth"], cell["rho"]
        factor = (-2.0 / 3.0) / (5.0 * rho * warmth * warmth)
        values = (
            cell["ux"], cell["uy"], cell["uz"], -0.5 / warmth, maxwell_scale(cell),
            cell["hx"] * factor, cell["hy"] * factor, cell["hz"] * factor,
        )
        for q, value in enumerate(values):
            for i in range(columns):
                coef[q, i] = spread(value, i, rows)

    depth = cell_ref[0, 0]
    for i in range(1, columns):
        depth = depth + cell_ref[0, i]
    diagonal = lane_index(rows) == lax.broadcasted_iota(jnp.int32, (rows, LANES), 0)
    depth_row = jnp.sum(jnp.where(diagonal, depth, 0.0), axis=0, keepdims=True)

    def block(b, carry):
        backward = lax.rem(octant_ref[step * blocks + b], 2)
        cx, cy, cz, neg_inv, wall = (
            table_row(base_ref, row, b, rows) for row in (CX, CY, CZ, NEG_INV, WALL)
        )
        gain = jnp.zeros((rows, LANES), F32)
        for s in range(columns):
            i = s + backward * (columns - 1 - 2 * s)
            px, py, pz = cx - coef[0, i], cy - coef[1, i], cz - coef[2, i]
            exponent = (px * px + py * py + pz * pz) * coef[3, i]
            skew = (px * coef[5, i] + py * coef[6, i] + pz * coef[7, i]) * (exponent + 2.5)
            target = coef[4, i] * jnp.exp(exponent) * (1.0 + skew)
            source = jnp.where(cell_ref[1, i] > 0.5, wall, target)
            attenuation = jnp.exp(cell_ref[0, i] * neg_inv)
            gain = attenuation * gain + (1.0 - attenuation) * source
            gain_ref[i, :, lane_block(b)] = gain
        message_ref[b, 0:rows] = gain
        message_ref[b, rows : rows + 1] = depth_row
        return carry

    lax.fori_loop(0, blocks, block, 0)


def entering_kernel(
    count, message_ref, base_ref, inflow_ref, out_ref,
    arrived, result, incoming, send_sem, recv_sem, back_send_sem, back_recv_sem,
):
    blocks = message_ref.shape[0]
    rows = inflow_ref.shape[1]
    me = lax.axis_index("gx")
    chip = lax.div(me, 2)
    is_owner = lax.rem(me, 2) == 0

    barrier = pltpu.get_barrier_semaphore()

    def greet(k, carry):
        pl.semaphore_signal(
            barrier, inc=1, device_id={"gx": lax.rem(me + k, count)}, device_id_type=MESH
        )
        return carry

    def greet_owner(k, carry):
        pl.semaphore_signal(
            barrier, inc=1, device_id={"gx": 2 * lax.rem(chip + k, blocks)}, device_id_type=MESH
        )
        return carry

    @pl.when(is_owner)
    def _():
        lax.fori_loop(1, count, greet, 0)
        pl.semaphore_wait(barrier, count - 1)

    @pl.when(jnp.logical_not(is_owner))
    def _():
        lax.fori_loop(0, blocks, greet_owner, 0)
        pl.semaphore_wait(barrier, blocks)

    def outgoing(b):
        return pltpu.make_async_remote_copy(
            src_ref=message_ref.at[b],
            dst_ref=arrived.at[me],
            send_sem=send_sem.at[b],
            recv_sem=recv_sem.at[me],
            device_id={"gx": 2 * b},
            device_id_type=MESH,
        )

    def start_out(k, carry):
        b = lax.rem(chip + k, blocks)

        @pl.when(2 * b != me)
        def _():
            outgoing(b).start()

        return carry

    lax.fori_loop(0, blocks, start_out, 0)

    def returning(j):
        return pltpu.make_async_remote_copy(
            src_ref=result.at[j],
            dst_ref=incoming.at[chip],
            send_sem=back_send_sem.at[j],
            recv_sem=back_recv_sem.at[chip],
            device_id={"gx": j},
            device_id_type=MESH,
        )

    @pl.when(is_owner)
    def _():
        arrived[me] = message_ref[chip]

        def wait_in(k, carry):
            j = lax.rem(me + k, count)
            pltpu.make_async_remote_copy(
                src_ref=message_ref.at[chip],
                dst_ref=arrived.at[j],
                send_sem=send_sem.at[chip],
                recv_sem=recv_sem.at[j],
                device_id={"gx": j},
                device_id_type=MESH,
            ).wait_recv()
            return carry

        lax.fori_loop(1, count, wait_in, 0)
        forward = table_row(base_ref, BACKWARD, chip, rows) < 0.5
        neg_inv = table_row(base_ref, NEG_INV, chip, rows)
        diagonal = lane_index(rows) == lax.broadcasted_iota(jnp.int32, (rows, LANES), 0)

        def lap(s, state):
            t = count - 1 - s
            gain = jnp.where(forward, arrived[s, 0:rows], arrived[t, 0:rows])
            depth_row = jnp.where(
                forward[0:1], arrived[s, rows : rows + 1], arrived[t, rows : rows + 1]
            )
            depth_all = jnp.broadcast_to(depth_row, (rows, LANES))
            depth = jnp.sum(jnp.where(diagonal, depth_all, 0.0), axis=1, keepdims=True)
            result[s] = state
            return jnp.exp(depth * neg_inv) * state + gain

        boundary = jnp.where(
            forward, inflow_ref[0, :, lane_block(chip)], inflow_ref[1, :, lane_block(chip)]
        )
        lax.fori_loop(0, count, lap, boundary, unroll=4)

        def flip(s, carry):
            t = count - 1 - s
            low, high = result[s], result[t]
            result[s] = jnp.where(forward, low, high)
            result[t] = jnp.where(forward, high, low)
            return carry

        lax.fori_loop(0, count // 2, flip, 0, unroll=4)

        def start_back(k, carry):
            returning(lax.rem(me + k, count)).start()
            return carry

        lax.fori_loop(1, count, start_back, 0)
        incoming[chip] = result[me]

    def wait_back(b, carry):
        @pl.when(2 * b != me)
        def _():
            pltpu.make_async_remote_copy(
                src_ref=result.at[0],
                dst_ref=incoming.at[b],
                send_sem=back_send_sem.at[0],
                recv_sem=back_recv_sem.at[b],
                device_id={"gx": 2 * b},
                device_id_type=MESH,
            ).wait_recv()

        return carry

    lax.fori_loop(0, blocks, wait_back, 0)
    out_ref[...] = incoming[...]

    def finish_out(b, carry):
        @pl.when(2 * b != me)
        def _():
            outgoing(b).wait_send()

        return carry

    lax.fori_loop(0, blocks, finish_out, 0)

    @pl.when(is_owner)
    def _():
        def finish_back(k, carry):
            returning(lax.rem(me + k, count)).wait_send()
            return carry

        lax.fori_loop(1, count, finish_back, 0)


def running_depth(cell_ref, depth_ref):
    columns = cell_ref.shape[1]
    total = cell_ref[0, 0]
    depth_ref[0, 0] = total
    for i in range(1, columns):
        total = total + cell_ref[0, i]
        depth_ref[0, i] = total
    total = cell_ref[0, columns - 1]
    depth_ref[1, columns - 1] = total
    for i in range(columns - 2, -1, -1):
        total = total + cell_ref[0, i]
        depth_ref[1, i] = total


def half_kernel(octant_ref, sums_ref, base_ref, cell_ref, gain_ref, enter_ref, out_ref, depth, totals):
    columns, rows, width = gain_ref.shape
    blocks = width // LANES
    step = pl.program_id(0)

    @pl.when(step == 0)
    def _():
        running_depth(cell_ref, depth)
        totals[...] = jnp.zeros_like(totals)

    def block(b, sums):
        backward = lax.rem(octant_ref[step * blocks + b], 2)
        neg_inv, weight, weight_e = (
            table_row(base_ref, row, b, rows) for row in (NEG_INV, WEIGHT, WEIGHT_E)
        )
        enter = enter_ref[b]
        sums = list(sums)
        for i in range(columns):
            decay = jnp.exp(depth[backward, i] * neg_inv)
            half = decay * enter + gain_ref[i, :, lane_block(b)]
            sums[i] = sums[i] + half * weight
            sums[columns + i] = sums[columns + i] + half * weight_e
        return tuple(sums)

    sums = tuple(totals[n] for n in range(2 * columns))
    sums = lax.fori_loop(0, blocks, block, sums)
    for n in range(2 * columns):
        totals[n] = sums[n]

    @pl.when(step == pl.num_programs(0) - 1)
    def _():
        cell = cell_values(sums_ref)
        lane = lane_index(rows)
        packed = jnp.zeros((rows, LANES), F32)
        for n, name in ((2, "warmth"), (3, "rho"), (4, "energy")):
            shifted = pltpu.roll(cell[name], 16 * n, 1)
            inside = jnp.logical_and(lane >= 16 * n, lane < 16 * n + 16)
            packed = jnp.where(inside, shifted, packed)
        for n in range(2 * columns):
            total = jnp.sum(sums[n], axis=1, keepdims=True)
            packed = jnp.where(lane == n, total, packed)
        out_ref[...] = packed


def halo_kernel(wide, count, mine_ref, out_ref, slots, send_sem, recv_sem):
    me = lax.axis_index("vert")
    col = lax.axis_index("gx")
    targets = [lax.rem(col + 1, wide), col, lax.rem(col + wide - 1, wide)]
    partners = [(side, k) for side in (0, 1, 2) for k in range(count) if (side, k) != (1, 0)]

    barrier = pltpu.get_barrier_semaphore()
    for side, k in partners:
        pl.semaphore_signal(
            barrier, inc=1,
            device_id={"gx": targets[side], "vert": lax.rem(me + k, count)},
            device_id_type=MESH,
        )
    pl.semaphore_wait(barrier, len(partners))

    def copy_to(side, k):
        return pltpu.make_async_remote_copy(
            src_ref=mine_ref,
            dst_ref=slots.at[side, me],
            send_sem=send_sem.at[side, k],
            recv_sem=recv_sem.at[side, me],
            device_id={"gx": targets[side], "vert": lax.rem(me + k, count)},
            device_id_type=MESH,
        )

    for side, k in partners:
        copy_to(side, k).start()
    slots[1, me] = mine_ref[...]
    for side, k in partners:
        other = lax.rem(me + k, count)
        pltpu.make_async_remote_copy(
            src_ref=mine_ref,
            dst_ref=slots.at[side, other],
            send_sem=send_sem.at[side, k],
            recv_sem=recv_sem.at[side, other],
            device_id={"gx": targets[2 - side], "vert": other},
            device_id_type=MESH,
        ).wait_recv()
    lane = lane_index(mine_ref.shape[0])
    for side in range(3):
        total = slots[side, 0]
        for k in range(1, count):
            total = total + slots[side, k]
        total = jnp.where(lane < 32, total, slots[side, 0])
        if side == 0:
            total = jnp.where(col == 0, 0.0, total)
        if side == 2:
            total = jnp.where(col == wide - 1, 0.0, total)
        out_ref[side] = total
    for side, k in partners:
        copy_to(side, k).wait_send()


def corrections(tiles_ref):
    rows = tiles_ref.shape[1]
    lane = lane_index(rows)
    row = lax.broadcasted_iota(jnp.int32, (rows, LANES), 0)

    def joined(n):
        def moved(side, start, place):
            shift = (place - 16 * n - start) % LANES
            return pltpu.roll(tiles_ref[side], shift, 1) if shift else tiles_ref[side]

        value = jnp.where(lane < 4, moved(0, 12, 0), moved(1, 0, 4))
        value = jnp.where(lane < 20, value, moved(2, 0, 20))
        return jnp.where(lane < 24, value, 0.0)

    warmth = joined(2)
    residuals = [joined(0) - joined(3), joined(1) - joined(4)]
    edges = (row == 0).astype(F32) + (row == rows - 1).astype(F32)
    scale = 1.0 / (1.0 + (4.0 - edges) * warmth)
    out = []
    for residual in residuals:
        value = residual * scale
        for _ in range(JAC):
            around = pltpu.roll(value, 1, 1) + pltpu.roll(value, LANES - 1, 1)
            around = around + jnp.where(row == 0, 0.0, pltpu.roll(value, 1, 0))
            around = around + jnp.where(row == rows - 1, 0.0, pltpu.roll(value, rows - 1, 0))
            value = (residual + warmth * around) * scale
        out.append(pltpu.roll(value, LANES - 4, 1))
    return out


def finish_kernel(
    octant_ref, tiles_ref, sums_ref, base_ref, cell_ref, gain_ref, enter_ref, out_ref, coef, depth
):
    columns, rows, width = gain_ref.shape
    blocks = width // LANES
    step = pl.program_id(0)

    @pl.when(step == 0)
    def _():
        running_depth(cell_ref, depth)
        cell = cell_values(sums_ref)
        rho, warmth = cell["rho"], cell["warmth"]
        change_rho, change_energy = corrections(tiles_ref)
        change_warmth = (
            2.0 * change_energy / 3.0 - (warmth + cell["flow_sq"] / 3.0) * change_rho
        ) / rho
        ratio_rho = change_rho / rho
        ratio_warmth = change_warmth / warmth
        scale = maxwell_scale(cell)
        values = (
            cell["ux"], cell["uy"], cell["uz"], -0.5 / warmth,
            scale * (ratio_rho - 1.5 * ratio_warmth), -(scale * ratio_warmth),
        )
        for q, value in enumerate(values):
            for i in range(columns):
                coef[q, i] = spread(value, i, rows)

    def block(b, carry):
        backward = lax.rem(octant_ref[step * blocks + b], 2)
        cx, cy, cz, neg_inv = (
            table_row(base_ref, row, b, rows) for row in (CX, CY, CZ, NEG_INV)
        )
        enter = enter_ref[b]
        for i in range(columns):
            px, py, pz = cx - coef[0, i], cy - coef[1, i], cz - coef[2, i]
            exponent = (px * px + py * py + pz * pz) * coef[3, i]
            decay = jnp.exp(depth[backward, i] * neg_inv)
            half = decay * enter + gain_ref[i, :, lane_block(b)]
            change = jnp.exp(exponent) * (coef[4, i] + coef[5, i] * exponent)
            out_ref[i, :, lane_block(b)] = half + change
        return carry

    lax.fori_loop(0, blocks, block, 0)


def velocity_table(speeds, jacobian, octant, wall_state):
    def over_lanes(sign):
        return jnp.broadcast_to(sign.astype(F32)[:, None], (octant.shape[0], LANES)).reshape(-1)

    cx = over_lanes(1 - 2 * (octant % 2)) * speeds[0]
    cy = over_lanes(1 - 2 * (octant // 2 % 2)) * speeds[1]
    cz = over_lanes(1 - 2 * (octant // 4)) * speeds[2]
    weight = jacobian * speeds[0] * speeds[1] * speeds[2] * (LOG_SPAN**3 / VEL)
    energy = weight * (0.5 * (cx * cx + cy * cy + cz * cz))
    return jnp.stack(
        [cx, cy, cz, weight, energy, -1.0 / speeds[0], wall_state, over_lanes(octant % 2)]
    )


def per_device(
    wide, count,
    prior_population, speeds, jacobian, octant, collision, solid_mask, wall_state, inflow,
):
    columns, rows, width = prior_population.shape
    blocks = width // LANES
    assert 2 * blocks == wide and columns == 16
    chunk = width // CHUNKS
    part = blocks // CHUNKS
    shape = jax.ShapeDtypeStruct
    whole = pl.BlockSpec(memory_space=pltpu.VMEM)
    scalars = pl.BlockSpec(memory_space=pltpu.SMEM)
    table_spec = pl.BlockSpec((8, chunk), lambda n: (0, n))
    field_spec = pl.BlockSpec((columns, rows, chunk), lambda n: (0, 0, n))
    tile_spec = pl.BlockSpec((part, rows, LANES), lambda n: (n, 0, 0))

    base = velocity_table(speeds, jacobian, octant, wall_state)
    solid = solid_mask == 1
    cell_in = jnp.stack([jnp.where(solid, SOLID_DEPTH, collision), solid.astype(F32)])
    cell_in = jnp.broadcast_to(cell_in[..., None], (2, columns, rows, LANES))

    partial = pl.pallas_call(
        moments_kernel,
        grid=(CHUNKS,),
        out_shape=shape((rows, 2 * LANES), F32),
        in_specs=[table_spec, field_spec],
        out_specs=whole,
        scratch_shapes=[
            pltpu.VMEM((MOMENTS, part, rows, LANES), F32),
            pltpu.VMEM((columns, MOMENTS, rows, LANES), F32),
        ],
    )(base, prior_population)

    sums = pl.pallas_call(
        functools.partial(vert_sum_kernel, count),
        out_shape=shape((rows, 2 * LANES), F32),
        in_specs=[whole],
        out_specs=whole,
        scratch_shapes=[
            pltpu.VMEM((count, rows, 2 * LANES), F32),
            pltpu.SemaphoreType.DMA((count,)),
            pltpu.SemaphoreType.DMA((count,)),
        ],
        compiler_params=pltpu.CompilerParams(collective_id=0, has_side_effects=True),
    )(partial)

    gains, messages = pl.pallas_call(
        sweep_kernel,
        grid=(CHUNKS,),
        out_shape=(shape((columns, rows, width), F32), shape((blocks, rows + 1, LANES), F32)),
        in_specs=[scalars, whole, table_spec, whole],
        out_specs=(field_spec, pl.BlockSpec((part, rows + 1, LANES), lambda n: (n, 0, 0))),
        scratch_shapes=[pltpu.VMEM((8, columns, rows, LANES), F32)],
    )(octant, sums, base, cell_in)

    enter = pl.pallas_call(
        functools.partial(entering_kernel, wide),
        out_shape=shape((blocks, rows, LANES), F32),
        in_specs=[whole, whole, whole],
        out_specs=whole,
        scratch_shapes=[
            pltpu.VMEM((wide, rows + 1, LANES), F32),
            pltpu.VMEM((wide, rows, LANES), F32),
            pltpu.VMEM((blocks, rows, LANES), F32),
            pltpu.SemaphoreType.DMA((blocks,)),
            pltpu.SemaphoreType.DMA((wide,)),
            pltpu.SemaphoreType.DMA((wide,)),
            pltpu.SemaphoreType.DMA((blocks,)),
        ],
        compiler_params=pltpu.CompilerParams(collective_id=1, has_side_effects=True),
    )(messages, base, inflow)

    tile = pl.pallas_call(
        half_kernel,
        grid=(CHUNKS,),
        out_shape=shape((rows, LANES), F32),
        in_specs=[scalars, whole, table_spec, whole, field_spec, tile_spec],
        out_specs=whole,
        scratch_shapes=[
            pltpu.VMEM((2, columns, rows, LANES), F32),
            pltpu.VMEM((2 * columns, rows, LANES), F32),
        ],
    )(octant, sums, base, cell_in, gains, enter)

    tiles = pl.pallas_call(
        functools.partial(halo_kernel, wide, count),
        out_shape=shape((3, rows, LANES), F32),
        in_specs=[whole],
        out_specs=whole,
        scratch_shapes=[
            pltpu.VMEM((3, count, rows, LANES), F32),
            pltpu.SemaphoreType.DMA((3, count)),
            pltpu.SemaphoreType.DMA((3, count)),
        ],
        compiler_params=pltpu.CompilerParams(collective_id=2, has_side_effects=True),
    )(tile)

    return pl.pallas_call(
        finish_kernel,
        grid=(CHUNKS,),
        out_shape=shape((columns, rows, width), F32),
        in_specs=[scalars, whole, whole, table_spec, whole, field_spec, tile_spec],
        out_specs=field_spec,
        scratch_shapes=[
            pltpu.VMEM((6, columns, rows, LANES), F32),
            pltpu.VMEM((2, columns, rows, LANES), F32),
        ],
    )(octant, tiles, sums, base, cell_in, gains, enter)


def solution(mesh):
    in_specs = (
        P("gx", None, "vert"),
        P(None, "vert"),
        P("vert"),
        P("vert"),
        P("gx", None),
        P("gx", None),
        P("vert"),
        P(None, None, "vert"),
    )
    return jax.shard_map(
        functools.partial(per_device, mesh.shape["gx"], mesh.shape["vert"]),
        mesh=mesh,
        in_specs=in_specs,
        out_specs=P("gx", None, "vert"),
        check_vma=False,
    )
```

time: 588 us -> 86.4 us (0.15)
  the two profiles are of different devices: /device:TPU:2 before, /device:TPU:1 now
where the time goes in v1:
time: 86.4 us; the launch traced here: 85.2 us
  Pallas kernels  78.6 us (91%)
  other arithmetic  3.92 us (5%)
  local copies, waits for them, and re-layouts  2.65 us (3%)
    pallas_call x1, Pallas kernels, per_device(): pl.pallas_call(functools.partial(entering_kernel, wide), out_shape=shape(...  34.5 us
    pallas_call x1, Pallas kernels, per_device(): pl.pallas_call(functools.partial(halo_kernel, wide, count), out_shape=sha...  12.8 us
    pallas_call x1, Pallas kernels, per_device(): pl.pallas_call(functools.partial(vert_sum_kernel, count), out_shape=shape...  10.6 us
    pallas_call x1, Pallas kernels, per_device(): pl.pallas_call(moments_kernel, grid=(CHUNKS,), out_shape=shape((rows, 2 *...  5.97 us
    pallas_call x1, Pallas kernels, per_device(): pl.pallas_call(finish_kernel, grid=(CHUNKS,), out_shape=shape((columns, r...  5.44 us
    pallas_call x1, Pallas kernels, per_device(): pl.pallas_call(sweep_kernel, grid=(CHUNKS,), out_shape=(shape((columns, r...  5.07 us
    pallas_call x1, Pallas kernels, per_device(): pl.pallas_call(half_kernel, grid=(CHUNKS,), out_shape=shape((rows, LANES)...  4.24 us

profile of v1, /device:TPU:1, one launch (start us, length us, event | category | flops | bytes accessed | tf_op | source)
XLA Modules:
  0.0 85.2 jit_solution(16566365771099833921)
XLA Ops:
  0.0 0.7 fusion.11
  0.7 0.7 subtract_convert_fusion
  1.3 0.7 select_bitcast_fusion
  2.1 0.1 copy.9
  2.1 0.1 broadcast_in_dim.16
  2.2 0.1 broadcast_in_dim.15
  2.3 0.1 broadcast_in_dim.14
  2.3 0.1 broadcast_in_dim.13
  2.4 1.1 %broadcast_divide_fusion = (f32[1,4096]{1,0:T(1,128)S(1)}, f32[1,4096]{1,0:T(1,128)S(1)}, f32[1,4096]{1,0:T(1,128)S(1)}, f32[1,4096]{1,0:T(1,128)S(1)}, f32[1,40...) fusion(f32[3,4096]{1,0:T(4,128)} %param.9, f32[1,4096]{1,0:T(1,128)S(1)} %bitcast.46, ...), kind=kLoop, calls=%fused_computation.12 | loop fusion | flops 16384 | bytes 212992 | tf_op jit(solution)/shard_map/div | solution.py:564
  3.5 0.8 fusion.3
  4.3 1.5 %stack.31.base_ref = f32[8,4096]{1,0:T(8,128)} concatenate(f32[1,4096]{1,0:T(1,128)S(1)} %get-tuple-element.14, f32[1,4096]{1,0:T(1,128)S(1)} %get-tuple-element.15, f32[1,4096]{1,0:T(1,128)S(1)} %get-tuple-element.16, f32[1,4096]{1,0:T(1,128)S(1)} %bitcast.39, f32[1,4096]{1,0:T(1,128)S(1)} %bitcast.38, f32[1,4096]{1,0:T(1,128)S(1)} %get-tuple-element.13, f32[1,4096]{1,0:T(1,128)} %bitcast.47, ...), dimensions={0} | concatenate | bytes 262144 | tf_op jit(solution)/shard_map/stack | solution.py:563
  5.8 6.0 %shard_map.82.mine_ref = f32[8,256]{1,0:T(8,128)} custom-call(f32[8,4096]{1,0:T(8,128)} %stack.31.base_ref, f32[16,8,4096]{2,1,0:T(8,128)} %prior_ref.1), custom_call_target="tpu_custom_call" | custom-call | tf_op jit(solution)/shard_map/pallas_call | solution.py:589
  11.8 10.6 %shard_map.83.sums_ref = f32[8,256]{1,0:T(8,128)} custom-call(f32[8,256]{1,0:T(8,128)} %shard_map.82.mine_ref), custom_call_target="tpu_custom_call" | custom-call | tf_op jit(solution)/shard_map/pallas_call | solution.py:601
  22.4 0.7 broadcast_in_dim.19.cell_ref
  23.1 5.1 %shard_map.84 = (f32[16,8,4096]{2,1,0:T(8,128)}, f32[32,9,128]{2,1,0:T(8,128)}) custom-call(s32[32]{0:T(128)} %octant_ref.5, f32[8,256]{1,0:T(8,128)} %shard_map.83.sums_ref, f32[8,4096]{1,0:T(8,128)} %stack.31.base_ref, f32[2,16,8,128]{3,2,1,0:T(8,128)} %broadcast_in_dim.19.cell_ref), custom_call_target="tpu_custom_call" | custom-call | tf_op jit(solution)/shard_map/pallas_call | solution.py:614
  28.2 34.5 %shard_map.85.enter_ref = f32[32,8,128]{2,1,0:T(8,128)} custom-call(f32[32,9,128]{2,1,0:T(8,128)} %get-tuple-element.8.message_ref, f32[8,4096]{1,0:T(8,128)} %stack.31.base_ref, f32[2,8,4096]{2,1,0:T(8,128)} %inflow_ref.1), custom_call_target="tpu_custom_call" | custom-call | tf_op jit(solution)/shard_map/pallas_call | solution.py:623
  62.7 4.2 %shard_map.86.mine_ref = f32[8,128]{1,0:T(8,128)} custom-call(s32[32]{0:T(128)} %octant_ref.5, f32[8,256]{1,0:T(8,128)} %shard_map.83.sums_ref, f32[8,4096]{1,0:T(8,128)} %stack.31.base_ref, f32[2,16,8,128]{3,2,1,0:T(8,128)} %broadcast_in_dim.19.cell_ref, f32[16,8,4096]{2,1,0:T(8,128)} %get-tuple-element.7.gain_ref, f32[32,8,128]{2,1,0:T(8,128)} %shard_map.85.enter_ref), custom_call_target="tpu_custom_call" | custom-call | tf_op jit(solution)/shard_map/pallas_call | solution.py:640
  67.0 12.8 %shard_map.87.tiles_ref = f32[3,8,128]{2,1,0:T(8,128)} custom-call(f32[8,128]{1,0:T(8,128)} %shard_map.86.mine_ref), custom_call_target="tpu_custom_call" | custom-call | tf_op jit(solution)/shard_map/pallas_call | solution.py:652
  79.8 5.4 %shard_map.88 = f32[16,8,4096]{2,1,0:T(8,128)} custom-call(s32[32]{0:T(128)} %octant_ref.5, f32[3,8,128]{2,1,0:T(8,128)} %shard_map.87.tiles_ref, f32[8,256]{1,0:T(8,128)} %shard_map.83.sums_ref, f32[8,4096]{1,0:T(8,128)} %stack.31.base_ref, f32[2,16,8,128]{3,2,1,0:T(8,128)} %broadcast_in_dim.19.cell_ref, f32[16,8,4096]{2,1,0:T(8,128)} %get-tuple-element.7.gain_ref, ...), custom_call_target="tpu_custom_call" | custom-call | tf_op jit(solution)/shard_map/pallas_call | solution.py:665
  (2 shorter events, 0.0 us)

commit v2 on v0

v2 whole, which is shorter than its diff:
```python
import functools
import math

import jax
import jax.numpy as jnp
from jax import lax
from jax.experimental import pallas as pl
from jax.experimental.pallas import tpu as pltpu
from jax.sharding import PartitionSpec as P

VEL = 32768
LANES = 128
JAC = 4
CHUNKS = 4
MOMENTS = 13
SOLID_DEPTH = 60.0
LOG_SPAN = 2.0 * math.log(60.0)
F32 = jnp.float32
MESH = pl.DeviceIdType.MESH

CX, CY, CZ, WEIGHT, WEIGHT_E, NEG_INV, WALL = range(7)


def lane_block(index):
    return pl.ds(pl.multiple_of(index * LANES, LANES), LANES)


def lane_index(rows):
    return lax.broadcasted_iota(jnp.int32, (rows, LANES), 1)


def row_index(rows):
    return lax.broadcasted_iota(jnp.int32, (rows, LANES), 0)


def velocity(speeds_ref, octant, block, rows):
    signs = (
        1 - 2 * lax.rem(octant, 2),
        1 - 2 * lax.rem(lax.div(octant, 2), 2),
        1 - 2 * lax.div(octant, 4),
    )
    return [
        jnp.broadcast_to(speeds_ref[n : n + 1, lane_block(block)], (rows, LANES)) * sign.astype(F32)
        for n, sign in enumerate(signs)
    ]


def cell_values(low, high):
    picked = []
    for m in range(MOMENTS):
        source = low if m < 8 else high
        shift = (LANES - 16 * (m % 8)) % LANES
        picked.append(pltpu.roll(source, shift, 1) if shift else source)
    valid = lane_index(low.shape[0]) < 16
    rho, sx, sy, sz, pxx, pxy, pxz, pyy, pyz, pzz, qx, qy, qz = (
        jnp.where(valid, value, 1.0) for value in picked
    )
    ux, uy, uz = sx / rho, sy / rho, sz / rho
    flow_sq = ux * ux + uy * uy + uz * uz
    second = pxx + pyy + pzz
    warmth = (second / rho - flow_sq) / 3.0
    swirl = rho * flow_sq
    heat_x = 0.5 * (qx - second * ux) - (ux * pxx + uy * pxy + uz * pxz) + swirl * ux
    heat_y = 0.5 * (qy - second * uy) - (ux * pxy + uy * pyy + uz * pyz) + swirl * uy
    heat_z = 0.5 * (qz - second * uz) - (ux * pxz + uy * pyz + uz * pzz) + swirl * uz
    return {
        "rho": rho, "ux": ux, "uy": uy, "uz": uz, "flow_sq": flow_sq, "warmth": warmth,
        "energy": 0.5 * second, "hx": heat_x, "hy": heat_y, "hz": heat_z,
    }


def maxwell_scale(cell):
    area = (2.0 * math.pi) * cell["warmth"]
    return cell["rho"] / (area * jnp.sqrt(area))


def spread(value, column, rows):
    return jnp.broadcast_to(value[:, column : column + 1], (rows, LANES))


def fused_kernel(
    wide, count, group_size,
    octant_ref, speeds_ref, jacobian_ref, wall_ref, collision_ref, solid_ref, inflow_ref, prior_ref,
    half_ref, tiles_ref, sums_ref,
    prior, table, moment, cells, att, decay, gain, coef, extra,
    mine, vert_slots, message, arrived, depths, prefix, joint, joint_slots,
    result, incoming, tile, halo_slots,
    prior_sem, vert_send, vert_recv, out_send, out_recv, joint_send, joint_recv,
    back_send, back_recv, halo_send, halo_recv,
):
    columns, rows, width = half_ref.shape
    blocks = width // LANES
    groups = wide // group_size
    me = lax.axis_index("vert")
    col = lax.axis_index("gx")
    group, pos = lax.div(col, group_size), lax.rem(col, group_size)
    diagonal = lane_index(rows) == row_index(rows)
    part = columns // CHUNKS

    def prior_copy(c):
        span = pl.ds(c * part, part)
        return pltpu.make_async_copy(prior_ref.at[span], prior.at[span], prior_sem.at[c])

    for c in range(CHUNKS):
        prior_copy(c).start()

    def in_vert(k):
        return {"vert": lax.rem(me + k, count)}

    def in_group(p):
        return {"gx": group * group_size + p}

    def in_joint(g):
        return {"gx": g * group_size + pos}

    sides = [lax.rem(col + 1, wide), col, lax.rem(col + wide - 1, wide)]
    halo_partners = [(side, k) for side in (0, 1, 2) for k in range(count) if (side, k) != (1, 0)]

    def in_halo(side, k):
        return {"gx": sides[side], "vert": lax.rem(me + k, count)}

    barrier = pltpu.get_barrier_semaphore()

    def greet(device):
        pl.semaphore_signal(barrier, inc=1, device_id=device, device_id_type=MESH)

    for side, k in halo_partners:
        greet(in_halo(side, k))
    for k in range(1, group_size):
        greet(in_group(lax.rem(pos + k, group_size)))
    for k in range(1, groups):
        greet(in_joint(lax.rem(group + k, groups)))

    def build(b, carry):
        cx, cy, cz = velocity(speeds_ref, octant_ref[b], b, rows)
        sx, sy, sz = (
            jnp.broadcast_to(speeds_ref[n : n + 1, lane_block(b)], (rows, LANES)) for n in range(3)
        )
        jac = jnp.broadcast_to(jacobian_ref[:, lane_block(b)], (rows, LANES))
        w = jac * sx * sy * sz * (LOG_SPAN**3 / VEL)
        square = cx * cx + cy * cy + cz * cz
        wx, wy, wz = w * cx, w * cy, w * cz
        table[CX, b] = cx
        table[CY, b] = cy
        table[CZ, b] = cz
        table[WEIGHT, b] = w
        table[WEIGHT_E, b] = w * (0.5 * square)
        table[NEG_INV, b] = -1.0 / sx
        table[WALL, b] = jnp.broadcast_to(wall_ref[:, lane_block(b)], (rows, LANES))
        entries = (
            w, wx, wy, wz,
            wx * cx, wx * cy, wx * cz, wy * cy, wy * cz, wz * cz,
            wx * square, wy * square, wz * square,
        )
        for m, entry in enumerate(entries):
            moment[m, b] = entry
        return carry

    lax.fori_loop(0, blocks, build, 0)

    square_eye = (
        lax.broadcasted_iota(jnp.int32, (rows, rows), 0)
        == lax.broadcasted_iota(jnp.int32, (rows, rows), 1)
    )

    def over_lanes(values):
        stacked = jnp.broadcast_to(values, (rows, rows))
        total = jnp.sum(jnp.where(square_eye, stacked, 0.0), axis=1, keepdims=True)
        return jnp.broadcast_to(total, (rows, LANES))

    total_depth = jnp.zeros((rows, LANES), F32)
    for i in range(columns):
        walled = solid_ref[i : i + 1, :] == 1
        cells[0, i] = over_lanes(jnp.where(walled, SOLID_DEPTH, collision_ref[i : i + 1, :]))
        cells[1, i] = over_lanes(jnp.where(walled, 1.0, 0.0))
        total_depth = total_depth + cells[0, i]
    depth_row = jnp.sum(jnp.where(diagonal, total_depth, 0.0), axis=0, keepdims=True)

    lane = lane_index(rows)

    def pair(g, packed):
        def add(b, sums):
            sums = list(sums)
            left = prior[2 * g, :, lane_block(b)]
            right = prior[2 * g + 1, :, lane_block(b)]
            for m in range(MOMENTS):
                entry = moment[m, b]
                sums[m] = sums[m] + left * entry
                sums[MOMENTS + m] = sums[MOMENTS + m] + right * entry
            return tuple(sums)

        zero = jnp.zeros((rows, LANES), F32)
        sums = lax.fori_loop(0, blocks, add, (zero,) * (2 * MOMENTS), unroll=4)
        packed = list(packed)
        for n in range(2 * MOMENTS):
            m = n % MOMENTS
            total = jnp.sum(sums[n], axis=1, keepdims=True)
            spot = lane == (m % 8) * 16 + 2 * g + n // MOMENTS
            packed[m // 8] = jnp.where(spot, total, packed[m // 8])
        return tuple(packed)

    def moment_chunk(c, packed):
        prior_copy(c).wait()
        return lax.fori_loop(c * (part // 2), (c + 1) * (part // 2), pair, packed)

    zero_tile = jnp.zeros((rows, LANES), F32)
    low, high = lax.fori_loop(0, CHUNKS, moment_chunk, (zero_tile, zero_tile))
    mine[:, :LANES] = low
    mine[:, LANES:] = high

    pl.semaphore_wait(barrier, len(halo_partners) + group_size - 1 + groups - 1)

    def vert_copy(k, slot):
        return pltpu.make_async_remote_copy(
            src_ref=mine, dst_ref=vert_slots.at[slot],
            send_sem=vert_send.at[k], recv_sem=vert_recv.at[slot],
            device_id=in_vert(k), device_id_type=MESH,
        )

    for k in range(1, count):
        vert_copy(k, me).start()

    def decays(b, carry):
        backward = lax.rem(octant_ref[b], 2)
        neg_inv = table[NEG_INV, b]
        running = jnp.ones((rows, LANES), F32)
        for s in range(columns):
            one = jnp.exp(cells[0, s + backward * (columns - 1 - 2 * s)] * neg_inv)
            running = running * one
            att[b, s] = one
            decay[b, s] = running
        return carry

    lax.fori_loop(0, blocks, decays, 0)

    vert_slots[me] = mine[...]
    for k in range(1, count):
        vert_copy(k, lax.rem(me + k, count)).wait_recv()
    total = vert_slots[0]
    for k in range(1, count):
        total = total + vert_slots[k]
    sums_ref[...] = total
    cell = cell_values(total[:, :LANES], total[:, LANES:])
    warmth, rho = cell["warmth"], cell["rho"]
    factor = (-2.0 / 3.0) / (5.0 * rho * warmth * warmth)
    values = (
        cell["ux"], cell["uy"], cell["uz"], -0.5 / warmth, maxwell_scale(cell),
        cell["hx"] * factor, cell["hy"] * factor, cell["hz"] * factor,
    )
    for q, value in enumerate(values):
        for i in range(columns):
            coef[q, i] = spread(value, i, rows)
    packed = zero_tile
    for n, name in ((2, "warmth"), (3, "rho"), (4, "energy")):
        inside = jnp.logical_and(lane >= 16 * n, lane < 16 * n + 16)
        packed = jnp.where(inside, pltpu.roll(cell[name], 16 * n, 1), packed)
    extra[...] = packed

    def out_copy(p, slot):
        return pltpu.make_async_remote_copy(
            src_ref=message.at[p], dst_ref=arrived.at[slot],
            send_sem=out_send.at[p], recv_sem=out_recv.at[slot],
            device_id=in_group(p), device_id_type=MESH,
        )

    def sweep(k, carry):
        p = lax.rem(pos + k, group_size)
        for q in range(2):
            b = 2 * p + q
            backward = lax.rem(octant_ref[b], 2)
            cx, cy, cz, wall = table[CX, b], table[CY, b], table[CZ, b], table[WALL, b]
            running = jnp.zeros((rows, LANES), F32)
            for s in range(columns):
                i = s + backward * (columns - 1 - 2 * s)
                px, py, pz = cx - coef[0, i], cy - coef[1, i], cz - coef[2, i]
                exponent = (px * px + py * py + pz * pz) * coef[3, i]
                skew = (px * coef[5, i] + py * coef[6, i] + pz * coef[7, i]) * (exponent + 2.5)
                target = coef[4, i] * jnp.exp(exponent) * (1.0 + skew)
                source = jnp.where(cells[1, i] > 0.5, wall, target)
                one = att[b, s]
                running = one * running + (1.0 - one) * source
                gain[b, s] = running
            message[p, q * rows : (q + 1) * rows] = running
        message[p, 2 * rows : 2 * rows + 1] = depth_row

        @pl.when(k < group_size)
        def _():
            out_copy(p, pos).start()

        return carry

    lax.fori_loop(1, group_size + 1, sweep, 0)
    arrived[pos] = message[pos]

    def wait_out(k, carry):
        out_copy(pos, lax.rem(pos + k, group_size)).wait_recv()
        return carry

    lax.fori_loop(1, group_size, wait_out, 0)

    for j in range(group_size):
        row = jnp.broadcast_to(arrived[j, 2 * rows : 2 * rows + 1], (rows, LANES))
        depth = jnp.sum(jnp.where(diagonal, row, 0.0), axis=1, keepdims=True)
        depths[j] = jnp.broadcast_to(depth, (rows, LANES))
    backwards = [lax.rem(octant_ref[2 * pos + q], 2) for q in range(2)]
    for q in range(2):
        neg_inv = table[NEG_INV, 2 * pos + q]
        kept, running = jnp.ones((rows, LANES), F32), jnp.zeros((rows, LANES), F32)
        for s in range(group_size):
            t = s + backwards[q] * (group_size - 1 - 2 * s)
            prefix[0, q, s] = kept
            prefix[1, q, s] = running
            one = jnp.exp(depths[t] * neg_inv)
            running = one * running + arrived[t, q * rows : (q + 1) * rows]
            kept = kept * one
        joint[q] = running
        joint[2 + q] = kept

    def joint_copy(g, slot):
        return pltpu.make_async_remote_copy(
            src_ref=joint, dst_ref=joint_slots.at[slot],
            send_sem=joint_send.at[g], recv_sem=joint_recv.at[slot],
            device_id=in_joint(g), device_id_type=MESH,
        )

    for k in range(1, groups):
        joint_copy(lax.rem(group + k, groups), group).start()
    joint_slots[group] = joint[...]
    for k in range(1, groups):
        joint_copy(group, lax.rem(group + k, groups)).wait_recv()
    entering = []
    for q in range(2):
        state = inflow_ref[backwards[q], :, lane_block(2 * pos + q)]
        place = group + backwards[q] * (groups - 1 - 2 * group)
        for s in range(groups - 1):
            g = s + backwards[q] * (groups - 1 - 2 * s)
            before = jnp.broadcast_to((place - s).astype(F32), (rows, LANES)) > 0.5
            longer = joint_slots[g, 2 + q] * state + joint_slots[g, q]
            state = jnp.where(before, longer, state)
        entering.append(state)

    def back_copy(j, slot):
        return pltpu.make_async_remote_copy(
            src_ref=result.at[j], dst_ref=incoming.at[slot],
            send_sem=back_send.at[j], recv_sem=back_recv.at[slot],
            device_id=in_group(j), device_id_type=MESH,
        )

    def send_back(k, carry):
        j = lax.rem(pos + k, group_size)
        for q in range(2):
            s = j + backwards[q] * (group_size - 1 - 2 * j)
            result[j, q] = prefix[0, q, s] * carry[q] + prefix[1, q, s]

        @pl.when(k < group_size)
        def _():
            back_copy(j, pos).start()

        return carry

    lax.fori_loop(1, group_size + 1, send_back, tuple(entering))
    incoming[pos] = result[pos]

    def halves(k, sums):
        p = lax.rem(pos + group_size - k, group_size)

        @pl.when(k > 0)
        def _():
            back_copy(pos, p).wait_recv()

        sums = list(sums)
        for q in range(2):
            b = 2 * p + q
            backward = lax.rem(octant_ref[b], 2)
            weight, weight_e = table[WEIGHT, b], table[WEIGHT_E, b]
            enter = incoming[p, q]
            for i in range(columns):
                s = i + backward * (columns - 1 - 2 * i)
                half = decay[b, s] * enter + gain[b, s]
                half_ref[i, :, lane_block(b)] = half
                sums[i] = sums[i] + half * weight
                sums[columns + i] = sums[columns + i] + half * weight_e
        return tuple(sums)

    sums = lax.fori_loop(0, group_size, halves, (zero_tile,) * (2 * columns))
    packed = extra[...]
    for n in range(2 * columns):
        packed = jnp.where(lane == n, jnp.sum(sums[n], axis=1, keepdims=True), packed)
    tile[...] = packed

    def halo_copy(side, k, slot):
        return pltpu.make_async_remote_copy(
            src_ref=tile, dst_ref=halo_slots.at[side, slot],
            send_sem=halo_send.at[side, k], recv_sem=halo_recv.at[side, slot],
            device_id=in_halo(side, k), device_id_type=MESH,
        )

    for side, k in halo_partners:
        halo_copy(side, k, me).start()
    halo_slots[1, me] = tile[...]
    for side, k in halo_partners:
        halo_copy(side, k, lax.rem(me + k, count)).wait_recv()
    for side in range(3):
        total = halo_slots[side, 0]
        for k in range(1, count):
            total = total + halo_slots[side, k]
        total = jnp.where(lane < 2 * columns, total, halo_slots[side, 0])
        if side == 0:
            total = jnp.where(col == 0, 0.0, total)
        if side == 2:
            total = jnp.where(col == wide - 1, 0.0, total)
        tiles_ref[side] = total

    for k in range(1, count):
        vert_copy(k, me).wait_send()
    for k in range(1, groups):
        joint_copy(lax.rem(group + k, groups), group).wait_send()

    def finish_sends(k, carry):
        p = lax.rem(pos + k, group_size)
        out_copy(p, pos).wait_send()
        back_copy(p, pos).wait_send()
        return carry

    lax.fori_loop(1, group_size, finish_sends, 0)
    for side, k in halo_partners:
        halo_copy(side, k, me).wait_send()


def corrections(tiles_ref):
    rows = tiles_ref.shape[1]
    lane, row = lane_index(rows), row_index(rows)

    def joined(n):
        def moved(side, start, place):
            shift = (place - 16 * n - start) % LANES
            return pltpu.roll(tiles_ref[side], shift, 1) if shift else tiles_ref[side]

        value = jnp.where(lane < 4, moved(0, 12, 0), moved(1, 0, 4))
        value = jnp.where(lane < 20, value, moved(2, 0, 20))
        return jnp.where(lane < 24, value, 0.0)

    warmth = joined(2)
    residuals = [joined(0) - joined(3), joined(1) - joined(4)]
    edges = (row == 0).astype(F32) + (row == rows - 1).astype(F32)
    scale = 1.0 / (1.0 + (4.0 - edges) * warmth)
    out = []
    for residual in residuals:
        value = residual * scale
        for _ in range(JAC):
            around = pltpu.roll(value, 1, 1) + pltpu.roll(value, LANES - 1, 1)
            around = around + jnp.where(row == 0, 0.0, pltpu.roll(value, 1, 0))
            around = around + jnp.where(row == rows - 1, 0.0, pltpu.roll(value, rows - 1, 0))
            value = (residual + warmth * around) * scale
        out.append(pltpu.roll(value, LANES - 4, 1))
    return out


def finish_kernel(octant_ref, tiles_ref, sums_ref, speeds_ref, half_ref, out_ref, coef):
    columns, rows, width = half_ref.shape
    blocks = width // LANES
    step = pl.program_id(0)

    @pl.when(step == 0)
    def _():
        cell = cell_values(sums_ref[:, :LANES], sums_ref[:, LANES:])
        rho, warmth = cell["rho"], cell["warmth"]
        change_rho, change_energy = corrections(tiles_ref)
        change_warmth = (
            2.0 * change_energy / 3.0 - (warmth + cell["flow_sq"] / 3.0) * change_rho
        ) / rho
        ratio_rho = change_rho / rho
        ratio_warmth = change_warmth / warmth
        scale = maxwell_scale(cell)
        values = (
            cell["ux"], cell["uy"], cell["uz"], -0.5 / warmth,
            scale * (ratio_rho - 1.5 * ratio_warmth), -(scale * ratio_warmth),
        )
        for q, value in enumerate(values):
            for i in range(columns):
                coef[q, i] = spread(value, i, rows)

    def block(b, carry):
        cx, cy, cz = velocity(speeds_ref, octant_ref[step * blocks + b], b, rows)
        for i in range(columns):
            px, py, pz = cx - coef[0, i], cy - coef[1, i], cz - coef[2, i]
            exponent = (px * px + py * py + pz * pz) * coef[3, i]
            change = jnp.exp(exponent) * (coef[4, i] + coef[5, i] * exponent)
            out_ref[i, :, lane_block(b)] = half_ref[i, :, lane_block(b)] + change
        return carry

    lax.fori_loop(0, blocks, block, 0)


def per_device(
    wide, count,
    prior_population, speeds, jacobian, octant, collision, solid_mask, wall_state, inflow,
):
    columns, rows, width = prior_population.shape
    blocks = width // LANES
    group_size = blocks // 2
    groups = wide // group_size
    assert groups * group_size == wide and columns == 16
    chunk = width // CHUNKS
    shape = jax.ShapeDtypeStruct
    whole = pl.BlockSpec(memory_space=pltpu.VMEM)
    scalars = pl.BlockSpec(memory_space=pltpu.SMEM)
    field_spec = pl.BlockSpec((columns, rows, chunk), lambda n: (0, 0, n))

    def tiles(*lead):
        return pltpu.VMEM(lead + (rows, LANES), F32)

    half, halo_tiles, sums = pl.pallas_call(
        functools.partial(fused_kernel, wide, count, group_size),
        out_shape=(
            shape((columns, rows, width), F32),
            shape((3, rows, LANES), F32),
            shape((rows, 2 * LANES), F32),
        ),
        in_specs=[scalars] + [whole] * 6 + [pl.BlockSpec(memory_space=pl.ANY)],
        out_specs=(whole, whole, whole),
        scratch_shapes=[
            pltpu.VMEM((columns, rows, width), F32),
            tiles(7, blocks),
            tiles(MOMENTS, blocks),
            tiles(2, columns),
            tiles(blocks, columns),
            tiles(blocks, columns),
            tiles(blocks, columns),
            tiles(8, columns),
            tiles(),
            pltpu.VMEM((rows, 2 * LANES), F32),
            pltpu.VMEM((count, rows, 2 * LANES), F32),
            pltpu.VMEM((group_size, 2 * rows + 1, LANES), F32),
            pltpu.VMEM((group_size, 2 * rows + 1, LANES), F32),
            tiles(group_size),
            tiles(2, 2, group_size),
            tiles(4),
            tiles(groups, 4),
            tiles(group_size, 2),
            tiles(group_size, 2),
            tiles(),
            tiles(3, count),
            pltpu.SemaphoreType.DMA((CHUNKS,)),
            pltpu.SemaphoreType.DMA((count,)),
            pltpu.SemaphoreType.DMA((count,)),
            pltpu.SemaphoreType.DMA((group_size,)),
            pltpu.SemaphoreType.DMA((group_size,)),
            pltpu.SemaphoreType.DMA((groups,)),
            pltpu.SemaphoreType.DMA((groups,)),
            pltpu.SemaphoreType.DMA((group_size,)),
            pltpu.SemaphoreType.DMA((group_size,)),
            pltpu.SemaphoreType.DMA((3, count)),
            pltpu.SemaphoreType.DMA((3, count)),
        ],
        compiler_params=pltpu.CompilerParams(
            collective_id=0, has_side_effects=True, vmem_limit_bytes=40 * 1024 * 1024
        ),
    )(
        octant, speeds, jacobian.reshape(1, width), wall_state.reshape(1, width),
        collision, solid_mask, inflow, prior_population,
    )

    return pl.pallas_call(
        finish_kernel,
        grid=(CHUNKS,),
        out_shape=shape((columns, rows, width), F32),
        in_specs=[
            scalars, whole, whole, pl.BlockSpec((3, chunk), lambda n: (0, n)), field_spec,
        ],
        out_specs=field_spec,
        scratch_shapes=[tiles(6, columns)],
    )(octant, halo_tiles, sums, speeds, half)


def solution(mesh):
    in_specs = (
        P("gx", None, "vert"),
        P(None, "vert"),
        P("vert"),
        P("vert"),
        P("gx", None),
        P("gx", None),
        P("vert"),
        P(None, None, "vert"),
    )
    return jax.shard_map(
        functools.partial(per_device, mesh.shape["gx"], mesh.shape["vert"]),
        mesh=mesh,
        in_specs=in_specs,
        out_specs=P("gx", None, "vert"),
        check_vma=False,
    )
```

time: 588 us -> 61.2 us (0.10)
  the two profiles are of different devices: /device:TPU:2 before, /device:TPU:1 now
where the time goes in v2:
time: 61.2 us; the launch traced here: 60.8 us
  Pallas kernels  51.2 us (84%)
  local copies, waits for them, and re-layouts  9.51 us (16%)
    pallas_call x1, Pallas kernels, per_device(): pl.pallas_call(functools.partial(fused_kernel, wide, count, group_size),...  46.1 us
    unnamed x20, local copies, waits for them, and re-layouts  9.51 us
    pallas_call x1, Pallas kernels, per_device(): pl.pallas_call(finish_kernel, grid=(CHUNKS,), out_shape=shape((columns, r...  5.16 us

profile of v2, /device:TPU:1, one launch (start us, length us, event | category | flops | bytes accessed | tf_op | source)
XLA Modules:
  0.0 60.8 jit_solution(4786822681505791128)
XLA Ops:
  0.0 0.8 %copy.9.collision_ref = f32[16,8]{1,0:T(8,128)S(1)} copy(f32[16,8]{0,1:T(8,128)} %param.12) | data formatting | bytes 1024 | tf_op args[4]
  0.8 0.8 %copy.10.solid_ref = s32[16,8]{1,0:T(8,128)S(1)} copy(s32[16,8]{0,1:T(8,128)} %param.13) | data formatting | bytes 1024 | tf_op args[5]
  1.5 0.0 copy-start
  1.5 1.6 %copy-done = f32[16,8,4096]{2,1,0:T(8,128)S(1)} copy-done((f32[16,8,4096]{2,1,0:T(8,128)S(1)}, f32[16,8,4096]{2,1,0:T(8,128)}, u32[]{:S(2)}) %copy-start) | copy-done | bytes 2097176
  3.1 0.0 copy-start.2
  3.1 0.9 %copy-done.2 = f32[2,8,4096]{2,1,0:T(8,128)S(1)} copy-done((f32[2,8,4096]{2,1,0:T(8,128)S(1)}, f32[2,8,4096]{2,1,0:T(8,128)}, u32[]{:S(2)}) %copy-start.2) | copy-done | bytes 262168
  4.1 0.0 copy-start.3
  4.1 0.8 %copy-done.3 = f32[3,4096]{1,0:T(4,128)S(1)} copy-done((f32[3,4096]{1,0:T(4,128)S(1)}, f32[3,4096]{1,0:T(4,128)}, u32[]{:S(2)}) %copy-start.3) | copy-done | bytes 49176
  4.9 0.0 copy-start.4
  4.9 0.7 %copy-done.4 = f32[4096]{0:T(1024)S(1)} copy-done((f32[4096]{0:T(1024)S(1)}, f32[4096]{0:T(1024)}, u32[]{:S(2)}) %copy-start.4) | copy-done | bytes 16408
  5.6 0.0 copy-start.5
  5.6 0.7 %copy-done.5 = f32[4096]{0:T(1024)S(1)} copy-done((f32[4096]{0:T(1024)S(1)}, f32[4096]{0:T(1024)}, u32[]{:S(2)}) %copy-start.5) | copy-done | bytes 16408
  6.3 0.0 copy-start.8
  6.3 0.7 %copy-done.8 = s32[32]{0:T(128)S(1)} copy-done((s32[32]{0:T(128)S(1)}, s32[32]{0:T(128)}, u32[]{:S(2)}) %copy-start.8) | copy-done | bytes 152
  7.0 46.1 %shard_map.82 = (f32[16,8,4096]{2,1,0:T(8,128)S(1)}, f32[3,8,128]{2,1,0:T(8,128)S(1)}, f32[8,256]{1,0:T(8,128)S(1)}) custom-call(s32[32]{0:T(128)S(1)} %copy-done.8, f32[3,4096]{1,0:T(4,128)S(1)} %copy-done.3, f32[1,4096]{1,0:T(1,128)S(1)} %bitcast.2, f32[1,4096]{1,0:T(1,128)S(1)} %bitcast.3, f32[16,8]{1,0:T(8,128)S(1)} %copy.9.collision_ref, ...), custom_call_target="tpu_custom_call" | custom-call | tf_op jit(solution)/shard_map/pallas_call | solution.py:513
  53.1 0.0 copy-start.1
  53.1 1.3 %copy-done.1 = f32[16,8,4096]{2,1,0:T(8,128)} copy-done((f32[16,8,4096]{2,1,0:T(8,128)}, f32[16,8,4096]{2,1,0:T(8,128)S(1)}, u32[]{:S(2)}) %copy-start.1) | copy-done | bytes 2097176
  54.4 0.0 copy-start.6
  54.4 0.6 copy-done.6
  55.0 0.0 copy-start.7
  55.0 0.6 copy-done.7
  55.6 5.2 %shard_map.83 = f32[16,8,4096]{2,1,0:T(8,128)} custom-call(s32[32]{0:T(128)} %octant_ref.3, f32[3,8,128]{2,1,0:T(8,128)} %copy-done.6, f32[8,256]{1,0:T(8,128)} %copy-done.7, f32[3,4096]{1,0:T(4,128)} %speeds_ref.3, f32[16,8,4096]{2,1,0:T(8,128)} %copy-done.1), custom_call_target="tpu_custom_call" | custom-call | tf_op jit(solution)/shard_map/pallas_call | solution.py:564
Async XLA Ops:
  1.5 1.6 %copy-start = (f32[16,8,4096]{2,1,0:T(8,128)S(1)}, f32[16,8,4096]{2,1,0:T(8,128)}, u32[]{:S(2)}) copy-start(f32[16,8,4096]{2,1,0:T(8,128)} %prior_ref.1) | copy-start | bytes 6291460
  3.1 0.9 %copy-start.2 = (f32[2,8,4096]{2,1,0:T(8,128)S(1)}, f32[2,8,4096]{2,1,0:T(8,128)}, u32[]{:S(2)}) copy-start(f32[2,8,4096]{2,1,0:T(8,128)} %inflow_ref.1) | copy-start | bytes 786436
  4.1 0.8 %copy-start.3 = (f32[3,4096]{1,0:T(4,128)S(1)}, f32[3,4096]{1,0:T(4,128)}, u32[]{:S(2)}) copy-start(f32[3,4096]{1,0:T(4,128)} %speeds_ref.3) | copy-start | bytes 147460
  4.9 0.7 %copy-start.4 = (f32[4096]{0:T(1024)S(1)}, f32[4096]{0:T(1024)}, u32[]{:S(2)}) copy-start(f32[4096]{0:T(1024)} %param.10) | copy-start | bytes 49156
  5.6 0.7 %copy-start.5 = (f32[4096]{0:T(1024)S(1)}, f32[4096]{0:T(1024)}, u32[]{:S(2)}) copy-start(f32[4096]{0:T(1024)} %param.14) | copy-start | bytes 49156
  6.3 0.7 %copy-start.8 = (s32[32]{0:T(128)S(1)}, s32[32]{0:T(128)}, u32[]{:S(2)}) copy-start(s32[32]{0:T(128)} %octant_ref.3) | copy-start | bytes 388
  53.1 1.3 %copy-start.1 = (f32[16,8,4096]{2,1,0:T(8,128)}, f32[16,8,4096]{2,1,0:T(8,128)S(1)}, u32[]{:S(2)}) copy-start(f32[16,8,4096]{2,1,0:T(8,128)S(1)} %get-tuple-element.10.half_ref) | copy-start | bytes 6291460
  54.4 0.6 copy-start.6
  55.0 0.6 copy-start.7

commit v3 on v2

--- a/solution.py
+++ b/solution.py
@@ -80,15 +80,16 @@
 
 def fused_kernel(
     wide, count, group_size,
-    octant_ref, speeds_ref, jacobian_ref, wall_ref, collision_ref, solid_ref, inflow_ref, prior_ref,
-    half_ref, tiles_ref, sums_ref,
-    prior, table, moment, cells, att, decay, gain, coef, extra,
+    octant_in, speeds_in, jacobian_in, wall_in, collision_in, solid_in, inflow_in, prior_in,
+    out_ref,
+    octant_ref, speeds_ref, jacobian_ref, wall_ref, collision_ref, solid_ref, inflow_ref, prior,
+    table, moment, totals, cells, att, decay, gain, power, bell, coef, extra, tiles_ref,
     mine, vert_slots, message, arrived, depths, prefix, joint, joint_slots,
     result, incoming, tile, halo_slots,
-    prior_sem, vert_send, vert_recv, out_send, out_recv, joint_send, joint_recv,
+    argument_sem, prior_sem, vert_send, vert_recv, out_send, out_recv, joint_send, joint_recv,
     back_send, back_recv, halo_send, halo_recv,
 ):
-    columns, rows, width = half_ref.shape
+    columns, rows, width = out_ref.shape
     blocks = width // LANES
     groups = wide // group_size
     me = lax.axis_index("vert")
@@ -99,10 +100,24 @@
 
     def prior_copy(c):
         span = pl.ds(c * part, part)
-        return pltpu.make_async_copy(prior_ref.at[span], prior.at[span], prior_sem.at[c])
-
+        return pltpu.make_async_copy(prior_in.at[span], prior.at[span], prior_sem.at[c])
+
+    owned = pl.ds(pl.multiple_of(pos * (2 * LANES), 2 * LANES), 2 * LANES)
+    pairs = (
+        (octant_in, octant_ref), (speeds_in, speeds_ref), (jacobian_in, jacobian_ref),
+        (wall_in, wall_ref), (collision_in, collision_ref), (solid_in, solid_ref),
+        (inflow_in.at[:, :, owned], inflow_ref),
+    )
+    arguments = [
+        pltpu.make_async_copy(source, target, argument_sem.at[n])
+        for n, (source, target) in enumerate(pairs)
+    ]
+    for copy in arguments[:3]:
+        copy.start()
     for c in range(CHUNKS):
         prior_copy(c).start()
+    for copy in arguments[3:]:
+        copy.start()
 
     def in_vert(k):
         return {"vert": lax.rem(me + k, count)}
@@ -130,6 +145,9 @@
         greet(in_group(lax.rem(pos + k, group_size)))
     for k in range(1, groups):
         greet(in_joint(lax.rem(group + k, groups)))
+
+    for copy in arguments[:3]:
+        copy.wait()
 
     def build(b, carry):
         cx, cy, cz = velocity(speeds_ref, octant_ref[b], b, rows)
@@ -145,8 +163,6 @@
         table[CZ, b] = cz
         table[WEIGHT, b] = w
         table[WEIGHT_E, b] = w * (0.5 * square)
-        table[NEG_INV, b] = -1.0 / sx
-        table[WALL, b] = jnp.broadcast_to(wall_ref[:, lane_block(b)], (rows, LANES))
         entries = (
             w, wx, wy, wz,
             wx * cx, wx * cy, wx * cz, wy * cy, wy * cz, wz * cz,
@@ -158,27 +174,11 @@
 
     lax.fori_loop(0, blocks, build, 0)
 
-    square_eye = (
-        lax.broadcasted_iota(jnp.int32, (rows, rows), 0)
-        == lax.broadcasted_iota(jnp.int32, (rows, rows), 1)
-    )
-
-    def over_lanes(values):
-        stacked = jnp.broadcast_to(values, (rows, rows))
-        total = jnp.sum(jnp.where(square_eye, stacked, 0.0), axis=1, keepdims=True)
-        return jnp.broadcast_to(total, (rows, LANES))
-
-    total_depth = jnp.zeros((rows, LANES), F32)
-    for i in range(columns):
-        walled = solid_ref[i : i + 1, :] == 1
-        cells[0, i] = over_lanes(jnp.where(walled, SOLID_DEPTH, collision_ref[i : i + 1, :]))
-        cells[1, i] = over_lanes(jnp.where(walled, 1.0, 0.0))
-        total_depth = total_depth + cells[0, i]
-    depth_row = jnp.sum(jnp.where(diagonal, total_depth, 0.0), axis=0, keepdims=True)
-
     lane = lane_index(rows)
 
-    def pair(g, packed):
+    zero_tile = jnp.zeros((rows, LANES), F32)
+
+    def pair(g, carry):
         def add(b, sums):
             sums = list(sums)
             left = prior[2 * g, :, lane_block(b)]
@@ -189,22 +189,28 @@
                 sums[MOMENTS + m] = sums[MOMENTS + m] + right * entry
             return tuple(sums)
 
-        zero = jnp.zeros((rows, LANES), F32)
-        sums = lax.fori_loop(0, blocks, add, (zero,) * (2 * MOMENTS), unroll=4)
+        sums = lax.fori_loop(0, blocks, add, (zero_tile,) * (2 * MOMENTS), unroll=4)
+        for m in range(MOMENTS):
+            totals[2 * g, m] = sums[m]
+            totals[2 * g + 1, m] = sums[MOMENTS + m]
+        return carry
+
+    def moment_chunk(c, carry):
+        prior_copy(c).wait()
+        return lax.fori_loop(c * (part // 2), (c + 1) * (part // 2), pair, carry)
+
+    lax.fori_loop(0, CHUNKS, moment_chunk, 0)
+
+    def pack(c, packed):
         packed = list(packed)
-        for n in range(2 * MOMENTS):
-            m = n % MOMENTS
-            total = jnp.sum(sums[n], axis=1, keepdims=True)
-            spot = lane == (m % 8) * 16 + 2 * g + n // MOMENTS
-            packed[m // 8] = jnp.where(spot, total, packed[m // 8])
+        for n in range(part):
+            for m in range(MOMENTS):
+                total = jnp.sum(totals[c * part + n, m], axis=1, keepdims=True)
+                spot = lane == (m % 8) * 16 + c * part + n
+                packed[m // 8] = jnp.where(spot, total, packed[m // 8])
         return tuple(packed)
 
-    def moment_chunk(c, packed):
-        prior_copy(c).wait()
-        return lax.fori_loop(c * (part // 2), (c + 1) * (part // 2), pair, packed)
-
-    zero_tile = jnp.zeros((rows, LANES), F32)
-    low, high = lax.fori_loop(0, CHUNKS, moment_chunk, (zero_tile, zero_tile))
+    low, high = lax.fori_loop(0, CHUNKS, pack, (zero_tile, zero_tile))
     mine[:, :LANES] = low
     mine[:, LANES:] = high
 
@@ -220,9 +226,24 @@
     for k in range(1, count):
         vert_copy(k, me).start()
 
+    for copy in arguments[3:]:
+        copy.wait()
+    walled = solid_ref[...] == 1
+    optical = jnp.where(walled, SOLID_DEPTH, collision_ref[...])
+    flags = jnp.where(walled, 1.0, 0.0)
+    total_depth = zero_tile
+    for i in range(columns):
+        cells[0, i] = spread(optical, i, rows)
+        cells[1, i] = spread(flags, i, rows)
+        total_depth = total_depth + cells[0, i]
+    depth_row = jnp.sum(jnp.where(diagonal, total_depth, 0.0), axis=0, keepdims=True)
+
     def decays(b, carry):
         backward = lax.rem(octant_ref[b], 2)
-        neg_inv = table[NEG_INV, b]
+        speed = jnp.broadcast_to(speeds_ref[0:1, lane_block(b)], (rows, LANES))
+        neg_inv = -1.0 / speed
+        table[NEG_INV, b] = neg_inv
+        table[WALL, b] = jnp.broadcast_to(wall_ref[:, lane_block(b)], (rows, LANES))
         running = jnp.ones((rows, LANES), F32)
         for s in range(columns):
             one = jnp.exp(cells[0, s + backward * (columns - 1 - 2 * s)] * neg_inv)
@@ -239,12 +260,12 @@
     total = vert_slots[0]
     for k in range(1, count):
         total = total + vert_slots[k]
-    sums_ref[...] = total
     cell = cell_values(total[:, :LANES], total[:, LANES:])
     warmth, rho = cell["warmth"], cell["rho"]
+    scale = maxwell_scale(cell)
     factor = (-2.0 / 3.0) / (5.0 * rho * warmth * warmth)
     values = (
-        cell["ux"], cell["uy"], cell["uz"], -0.5 / warmth, maxwell_scale(cell),
+        cell["ux"], cell["uy"], cell["uz"], -0.5 / warmth, scale,
         cell["hx"] * factor, cell["hy"] * factor, cell["hz"] * factor,
     )
     for q, value in enumerate(values):
@@ -254,7 +275,9 @@
     for n, name in ((2, "warmth"), (3, "rho"), (4, "energy")):
         inside = jnp.logical_and(lane >= 16 * n, lane < 16 * n + 16)
         packed = jnp.where(inside, pltpu.roll(cell[name], 16 * n, 1), packed)
-    extra[...] = packed
+    extra[0] = packed
+    for n, value in enumerate((rho, warmth, cell["flow_sq"], scale)):
+        extra[1 + n] = value
 
     def out_copy(p, slot):
         return pltpu.make_async_remote_copy(
@@ -275,7 +298,10 @@
                 px, py, pz = cx - coef[0, i], cy - coef[1, i], cz - coef[2, i]
                 exponent = (px * px + py * py + pz * pz) * coef[3, i]
                 skew = (px * coef[5, i] + py * coef[6, i] + pz * coef[7, i]) * (exponent + 2.5)
-                target = coef[4, i] * jnp.exp(exponent) * (1.0 + skew)
+                weight = jnp.exp(exponent)
+                power[b, s] = exponent
+                bell[b, s] = weight
+                target = coef[4, i] * weight * (1.0 + skew)
                 source = jnp.where(cells[1, i] > 0.5, wall, target)
                 one = att[b, s]
                 running = one * running + (1.0 - one) * source
@@ -330,7 +356,7 @@
         joint_copy(group, lax.rem(group + k, groups)).wait_recv()
     entering = []
     for q in range(2):
-        state = inflow_ref[backwards[q], :, lane_block(2 * pos + q)]
+        state = inflow_ref[backwards[q], :, q * LANES : (q + 1) * LANES]
         place = group + backwards[q] * (groups - 1 - 2 * group)
         for s in range(groups - 1):
             g = s + backwards[q] * (groups - 1 - 2 * s)
@@ -377,13 +403,13 @@
             for i in range(columns):
                 s = i + backward * (columns - 1 - 2 * i)
                 half = decay[b, s] * enter + gain[b, s]
-                half_ref[i, :, lane_block(b)] = half
+                out_ref[i, :, lane_block(b)] = half
                 sums[i] = sums[i] + half * weight
                 sums[columns + i] = sums[columns + i] + half * weight_e
         return tuple(sums)
 
     sums = lax.fori_loop(0, group_size, halves, (zero_tile,) * (2 * columns))
-    packed = extra[...]
+    packed = extra[0]
     for n in range(2 * columns):
         packed = jnp.where(lane == n, jnp.sum(sums[n], axis=1, keepdims=True), packed)
     tile[...] = packed
@@ -411,6 +437,25 @@
             total = jnp.where(col == wide - 1, 0.0, total)
         tiles_ref[side] = total
 
+    rho, warmth, flow_sq, scale = (extra[1 + n] for n in range(4))
+    change_rho, change_energy = corrections(tiles_ref)
+    change_warmth = (2.0 * change_energy / 3.0 - (warmth + flow_sq / 3.0) * change_rho) / rho
+    ratio_rho = change_rho / rho
+    ratio_warmth = change_warmth / warmth
+    for q, value in enumerate((scale * (ratio_rho - 1.5 * ratio_warmth), -(scale * ratio_warmth))):
+        for i in range(columns):
+            coef[q, i] = spread(value, i, rows)
+
+    def finish(b, carry):
+        backward = lax.rem(octant_ref[b], 2)
+        for i in range(columns):
+            s = i + backward * (columns - 1 - 2 * i)
+            change = bell[b, s] * (coef[0, i] + coef[1, i] * power[b, s])
+            out_ref[i, :, lane_block(b)] = out_ref[i, :, lane_block(b)] + change
+        return carry
+
+    lax.fori_loop(0, blocks, finish, 0)
+
     for k in range(1, count):
         vert_copy(k, me).wait_send()
     for k in range(1, groups):
@@ -456,42 +501,6 @@
     return out
 
 
-def finish_kernel(octant_ref, tiles_ref, sums_ref, speeds_ref, half_ref, out_ref, coef):
-    columns, rows, width = half_ref.shape
-    blocks = width // LANES
-    step = pl.program_id(0)
-
-    @pl.when(step == 0)
-    def _():
-        cell = cell_values(sums_ref[:, :LANES], sums_ref[:, LANES:])
-        rho, warmth = cell["rho"], cell["warmth"]
-        change_rho, change_energy = corrections(tiles_ref)
-        change_warmth = (
-            2.0 * change_energy / 3.0 - (warmth + cell["flow_sq"] / 3.0) * change_rho
-        ) / rho
-        ratio_rho = change_rho / rho
-        ratio_warmth = change_warmth / warmth
-        scale = maxwell_scale(cell)
-        values = (
-            cell["ux"], cell["uy"], cell["uz"], -0.5 / warmth,
-            scale * (ratio_rho - 1.5 * ratio_warmth), -(scale * ratio_warmth),
-        )
-        for q, value in enumerate(values):
-            for i in range(columns):
-                coef[q, i] = spread(value, i, rows)
-
-    def block(b, carry):
-        cx, cy, cz = velocity(speeds_ref, octant_ref[step * blocks + b], b, rows)
-        for i in range(columns):
-            px, py, pz = cx - coef[0, i], cy - coef[1, i], cz - coef[2, i]
-            exponent = (px * px + py * py + pz * pz) * coef[3, i]
-            change = jnp.exp(exponent) * (coef[4, i] + coef[5, i] * exponent)
-            out_ref[i, :, lane_block(b)] = half_ref[i, :, lane_block(b)] + change
-        return carry
-
-    lax.fori_loop(0, blocks, block, 0)
-
-
 def per_device(
     wide, count,
     prior_population, speeds, jacobian, octant, collision, solid_mask, wall_state, inflow,
@@ -501,34 +510,48 @@
     group_size = blocks // 2
     groups = wide // group_size
     assert groups * group_size == wide and columns == 16
-    chunk = width // CHUNKS
     shape = jax.ShapeDtypeStruct
-    whole = pl.BlockSpec(memory_space=pltpu.VMEM)
-    scalars = pl.BlockSpec(memory_space=pltpu.SMEM)
-    field_spec = pl.BlockSpec((columns, rows, chunk), lambda n: (0, 0, n))
+    stays = pl.BlockSpec(memory_space=pltpu.HBM)
 
     def tiles(*lead):
         return pltpu.VMEM(lead + (rows, LANES), F32)
 
-    half, halo_tiles, sums = pl.pallas_call(
+    def dma(*counts):
+        return pltpu.SemaphoreType.DMA(counts)
+
+    arguments = [
+        pltpu.with_memory_space_constraint(value, pltpu.HBM)
+        for value in (
+            octant, speeds, jacobian.reshape(1, width), wall_state.reshape(1, width),
+            collision.T, solid_mask.T, inflow, prior_population,
+        )
+    ]
+    return pl.pallas_call(
         functools.partial(fused_kernel, wide, count, group_size),
-        out_shape=(
-            shape((columns, rows, width), F32),
-            shape((3, rows, LANES), F32),
-            shape((rows, 2 * LANES), F32),
-        ),
-        in_specs=[scalars] + [whole] * 6 + [pl.BlockSpec(memory_space=pl.ANY)],
-        out_specs=(whole, whole, whole),
+        out_shape=shape((columns, rows, width), F32),
+        in_specs=[stays] * 8,
+        out_specs=pl.BlockSpec(memory_space=pltpu.VMEM),
         scratch_shapes=[
+            pltpu.SMEM((blocks,), jnp.int32),
+            pltpu.VMEM((3, width), F32),
+            pltpu.VMEM((1, width), F32),
+            pltpu.VMEM((1, width), F32),
+            pltpu.VMEM((rows, columns), F32),
+            pltpu.VMEM((rows, columns), jnp.int32),
+            pltpu.VMEM((2, rows, 2 * LANES), F32),
             pltpu.VMEM((columns, rows, width), F32),
             tiles(7, blocks),
             tiles(MOMENTS, blocks),
+            tiles(columns, MOMENTS),
             tiles(2, columns),
             tiles(blocks, columns),
             tiles(blocks, columns),
             tiles(blocks, columns),
+            tiles(blocks, columns),
+            tiles(blocks, columns),
             tiles(8, columns),
-            tiles(),
+            tiles(5),
+            tiles(3),
             pltpu.VMEM((rows, 2 * LANES), F32),
             pltpu.VMEM((count, rows, 2 * LANES), F32),
             pltpu.VMEM((group_size, 2 * rows + 1, LANES), F32),
@@ -541,36 +564,14 @@
             tiles(group_size, 2),
             tiles(),
             tiles(3, count),
-            pltpu.SemaphoreType.DMA((CHUNKS,)),
-            pltpu.SemaphoreType.DMA((count,)),
-            pltpu.SemaphoreType.DMA((count,)),
-            pltpu.SemaphoreType.DMA((group_size,)),
-            pltpu.SemaphoreType.DMA((group_size,)),
-            pltpu.SemaphoreType.DMA((groups,)),
-            pltpu.SemaphoreType.DMA((groups,)),
-            pltpu.SemaphoreType.DMA((group_size,)),
-            pltpu.SemaphoreType.DMA((group_size,)),
-            pltpu.SemaphoreType.DMA((3, count)),
-            pltpu.SemaphoreType.DMA((3, count)),
+            dma(7), dma(CHUNKS), dma(count), dma(count), dma(group_size), dma(group_size),
+            dma(groups), dma(groups), dma(group_size), dma(group_size),
+            dma(3, count), dma(3, count),
         ],
         compiler_params=pltpu.CompilerParams(
             collective_id=0, has_side_effects=True, vmem_limit_bytes=40 * 1024 * 1024
         ),
-    )(
-        octant, speeds, jacobian.reshape(1, width), wall_state.reshape(1, width),
-        collision, solid_mask, inflow, prior_population,
-    )
-
-    return pl.pallas_call(
-        finish_kernel,
-        grid=(CHUNKS,),
-        out_shape=shape((columns, rows, width), F32),
-        in_specs=[
-            scalars, whole, whole, pl.BlockSpec((3, chunk), lambda n: (0, n)), field_spec,
-        ],
-        out_specs=field_spec,
-        scratch_shapes=[tiles(6, columns)],
-    )(octant, halo_tiles, sums, speeds, half)
+    )(*arguments)
 
 
 def solution(mesh):

time: 61.2 us -> 48.5 us (0.79)
  local copies, waits for them, and re-layouts: 9.51 us -> 1.32 us
  Pallas kernels: 51.2 us -> 47 us
    unnamed x20 -> x1, local copies, waits for them, and re-layouts: 9.51 us -> 1.32 us
    pallas_call x1 -> x0, Pallas kernels: 5.16 us -> none  [per_device(): pl.pallas_call(finish_kernel, grid=(CHUNKS,), out_shape=shape((columns, r...]
    pallas_call x1, Pallas kernels: 46.1 us -> 47 us  [per_device(): pl.pallas_call(functools.partial(fused_kernel, wide, count, group_size),...]
where the time goes in v3:
time: 48.5 us; the launch traced here: 48.4 us
  Pallas kernels  47 us (97%)
  local copies, waits for them, and re-layouts  1.32 us (3%)
    pallas_call x1, Pallas kernels, per_device(): pl.pallas_call(functools.partial(fused_kernel, wide, count, group_size),...  47 us
    unnamed x1, local copies, waits for them, and re-layouts  1.32 us

profile of v3, /device:TPU:1, one launch (start us, length us, event | category | flops | bytes accessed | tf_op | source)
XLA Modules:
  0.0 48.4 jit_solution(1262412684491811658)
XLA Ops:
  0.0 47.0 %shard_map.82 = f32[16,8,4096]{2,1,0:T(8,128)S(1)} custom-call(s32[32]{0:T(128)} %octant_in.1, f32[3,4096]{1,0:T(4,128)} %speeds_in.1, f32[1,4096]{1,0:T(1,128)} %bitcast.4, f32[1,4096]{1,0:T(1,128)} %bitcast.5, f32[8,16]{1,0:T(8,128)} %bitcast.6, s32[8,16]{1,0:T(8,128)} %bitcast.7, f32[2,8,4096]{2,1,0:T(8,128)} %inflow_in.1, f32[16,8,4096]{2,1,0:T(8,128)} %prior_in.1), custom_call_target="tpu_custom_call" | custom-call | tf_op jit(solution)/shard_map/pallas_call | solution.py:529
  47.0 1.3 %copy.10 = f32[16,8,4096]{2,1,0:T(8,128)} copy(f32[16,8,4096]{2,1,0:T(8,128)S(1)} %shard_map.82) | data formatting | bytes 4194304

commit v4 on v3

--- a/solution.py
+++ b/solution.py
@@ -83,7 +83,7 @@
     octant_in, speeds_in, jacobian_in, wall_in, collision_in, solid_in, inflow_in, prior_in,
     out_ref,
     octant_ref, speeds_ref, jacobian_ref, wall_ref, collision_ref, solid_ref, inflow_ref, prior,
-    table, moment, totals, cells, att, decay, gain, power, bell, coef, extra, tiles_ref,
+    table, moment, totals, cells, att, decay, gain, power, bell, coef, extra, half_sums, tiles_ref,
     mine, vert_slots, message, arrived, depths, prefix, joint, joint_slots,
     result, incoming, tile, halo_slots,
     argument_sem, prior_sem, vert_send, vert_recv, out_send, out_recv, joint_send, joint_recv,
@@ -318,6 +318,20 @@
     lax.fori_loop(1, group_size + 1, sweep, 0)
     arrived[pos] = message[pos]
 
+    def gain_sums(b, sums):
+        backward = lax.rem(octant_ref[b], 2)
+        weight, weight_e = table[WEIGHT, b], table[WEIGHT_E, b]
+        sums = list(sums)
+        for i in range(columns):
+            value = gain[b, i + backward * (columns - 1 - 2 * i)]
+            sums[i] = sums[i] + value * weight
+            sums[columns + i] = sums[columns + i] + value * weight_e
+        return tuple(sums)
+
+    sums = lax.fori_loop(0, blocks, gain_sums, (zero_tile,) * (2 * columns))
+    for n in range(2 * columns):
+        half_sums[n] = sums[n]
+
     def wait_out(k, carry):
         out_copy(pos, lax.rem(pos + k, group_size)).wait_recv()
         return carry
@@ -402,13 +416,13 @@
             enter = incoming[p, q]
             for i in range(columns):
                 s = i + backward * (columns - 1 - 2 * i)
-                half = decay[b, s] * enter + gain[b, s]
-                out_ref[i, :, lane_block(b)] = half
-                sums[i] = sums[i] + half * weight
-                sums[columns + i] = sums[columns + i] + half * weight_e
+                value = decay[b, s] * enter
+                sums[i] = sums[i] + value * weight
+                sums[columns + i] = sums[columns + i] + value * weight_e
         return tuple(sums)
 
-    sums = lax.fori_loop(0, group_size, halves, (zero_tile,) * (2 * columns))
+    sums = tuple(half_sums[n] for n in range(2 * columns))
+    sums = lax.fori_loop(0, group_size, halves, sums)
     packed = extra[0]
     for n in range(2 * columns):
         packed = jnp.where(lane == n, jnp.sum(sums[n], axis=1, keepdims=True), packed)
@@ -424,6 +438,32 @@
     for side, k in halo_partners:
         halo_copy(side, k, me).start()
     halo_slots[1, me] = tile[...]
+
+    def form(b, carry):
+        backward = lax.rem(octant_ref[b], 2)
+        enter = incoming[lax.div(b, 2), lax.rem(b, 2)]
+        for i in range(columns):
+            s = i + backward * (columns - 1 - 2 * i)
+            out_ref[i, :, lane_block(b)] = decay[b, s] * enter + gain[b, s]
+        return carry
+
+    lax.fori_loop(0, blocks, form, 0)
+
+    for k in range(1, count):
+        vert_copy(k, me).wait_send()
+    for k in range(1, groups):
+        joint_copy(lax.rem(group + k, groups), group).wait_send()
+
+    def finish_sends(k, carry):
+        p = lax.rem(pos + k, group_size)
+        out_copy(p, pos).wait_send()
+        back_copy(p, pos).wait_send()
+        return carry
+
+    lax.fori_loop(1, group_size, finish_sends, 0)
+    for side, k in halo_partners:
+        halo_copy(side, k, me).wait_send()
+
     for side, k in halo_partners:
         halo_copy(side, k, lax.rem(me + k, count)).wait_recv()
     for side in range(3):
@@ -442,34 +482,24 @@
     change_warmth = (2.0 * change_energy / 3.0 - (warmth + flow_sq / 3.0) * change_rho) / rho
     ratio_rho = change_rho / rho
     ratio_warmth = change_warmth / warmth
-    for q, value in enumerate((scale * (ratio_rho - 1.5 * ratio_warmth), -(scale * ratio_warmth))):
-        for i in range(columns):
-            coef[q, i] = spread(value, i, rows)
-
-    def finish(b, carry):
-        backward = lax.rem(octant_ref[b], 2)
-        for i in range(columns):
-            s = i + backward * (columns - 1 - 2 * i)
-            change = bell[b, s] * (coef[0, i] + coef[1, i] * power[b, s])
-            out_ref[i, :, lane_block(b)] = out_ref[i, :, lane_block(b)] + change
-        return carry
-
-    lax.fori_loop(0, blocks, finish, 0)
-
-    for k in range(1, count):
-        vert_copy(k, me).wait_send()
-    for k in range(1, groups):
-        joint_copy(lax.rem(group + k, groups), group).wait_send()
-
-    def finish_sends(k, carry):
-        p = lax.rem(pos + k, group_size)
-        out_copy(p, pos).wait_send()
-        back_copy(p, pos).wait_send()
-        return carry
-
-    lax.fori_loop(1, group_size, finish_sends, 0)
-    for side, k in halo_partners:
-        halo_copy(side, k, me).wait_send()
+    level, slope = scale * (ratio_rho - 1.5 * ratio_warmth), -(scale * ratio_warmth)
+
+    def finish_columns(low, high):
+        levels = [spread(level, i, rows) for i in range(low, high)]
+        slopes = [spread(slope, i, rows) for i in range(low, high)]
+
+        def finish(b, carry):
+            backward = lax.rem(octant_ref[b], 2)
+            for n, i in enumerate(range(low, high)):
+                s = i + backward * (columns - 1 - 2 * i)
+                change = bell[b, s] * (levels[n] + slopes[n] * power[b, s])
+                out_ref[i, :, lane_block(b)] = out_ref[i, :, lane_block(b)] + change
+            return carry
+
+        lax.fori_loop(0, blocks, finish, 0)
+
+    finish_columns(0, columns // 2)
+    finish_columns(columns // 2, columns)
 
 
 def corrections(tiles_ref):
@@ -551,6 +581,7 @@
             tiles(blocks, columns),
             tiles(8, columns),
             tiles(5),
+            tiles(2 * columns),
             tiles(3),
             pltpu.VMEM((rows, 2 * LANES), F32),
             pltpu.VMEM((count, rows, 2 * LANES), F32),

time: 48.5 us -> 48.6 us (level)
  no operation moved by 1% of the time
where the time goes in v4:
time: 48.6 us; the launch traced here: 48.4 us
  Pallas kernels  47.1 us (97%)
  local copies, waits for them, and re-layouts  1.32 us (3%)
    pallas_call x1, Pallas kernels, per_device(): pl.pallas_call(functools.partial(fused_kernel, wide, count, group_size),...  47.1 us
    unnamed x1, local copies, waits for them, and re-layouts  1.32 us

profile of v4, /device:TPU:1, one launch (start us, length us, event | category | flops | bytes accessed | tf_op | source)
XLA Modules:
  0.0 48.4 jit_solution(18187597865936201263)
XLA Ops:
  0.0 47.1 %shard_map.82 = f32[16,8,4096]{2,1,0:T(8,128)S(1)} custom-call(s32[32]{0:T(128)} %octant_in.1, f32[3,4096]{1,0:T(4,128)} %speeds_in.1, f32[1,4096]{1,0:T(1,128)} %bitcast.4, f32[1,4096]{1,0:T(1,128)} %bitcast.5, f32[8,16]{1,0:T(8,128)} %bitcast.6, s32[8,16]{1,0:T(8,128)} %bitcast.7, f32[2,8,4096]{2,1,0:T(8,128)} %inflow_in.1, f32[16,8,4096]{2,1,0:T(8,128)} %prior_in.1), custom_call_target="tpu_custom_call" | custom-call | tf_op jit(solution)/shard_map/pallas_call | solution.py:559
  47.1 1.3 %copy.10 = f32[16,8,4096]{2,1,0:T(8,128)} copy(f32[16,8,4096]{2,1,0:T(8,128)S(1)} %shard_map.82) | data formatting | bytes 4194304

commit v5 on v4

--- a/solution.py
+++ b/solution.py
@@ -85,13 +85,14 @@
     octant_ref, speeds_ref, jacobian_ref, wall_ref, collision_ref, solid_ref, inflow_ref, prior,
     table, moment, totals, cells, att, decay, gain, power, bell, coef, extra, half_sums, tiles_ref,
     mine, vert_slots, message, arrived, depths, prefix, joint, joint_slots,
-    result, incoming, tile, halo_slots,
+    result, incoming, tile, tile_slots, line_slots,
     argument_sem, prior_sem, vert_send, vert_recv, out_send, out_recv, joint_send, joint_recv,
-    back_send, back_recv, halo_send, halo_recv,
+    back_send, back_recv, tile_send, tile_recv, line_send, line_recv,
 ):
     columns, rows, width = out_ref.shape
     blocks = width // LANES
     groups = wide // group_size
+    own = blocks // group_size
     me = lax.axis_index("vert")
     col = lax.axis_index("gx")
     group, pos = lax.div(col, group_size), lax.rem(col, group_size)
@@ -102,7 +103,7 @@
         span = pl.ds(c * part, part)
         return pltpu.make_async_copy(prior_in.at[span], prior.at[span], prior_sem.at[c])
 
-    owned = pl.ds(pl.multiple_of(pos * (2 * LANES), 2 * LANES), 2 * LANES)
+    owned = pl.ds(pl.multiple_of(pos * (own * LANES), LANES), own * LANES)
     pairs = (
         (octant_in, octant_ref), (speeds_in, speeds_ref), (jacobian_in, jacobian_ref),
         (wall_in, wall_ref), (collision_in, collision_ref), (solid_in, solid_ref),
@@ -122,29 +123,38 @@
     def in_vert(k):
         return {"vert": lax.rem(me + k, count)}
 
-    def in_group(p):
-        return {"gx": group * group_size + p}
-
-    def in_joint(g):
-        return {"gx": g * group_size + pos}
-
-    sides = [lax.rem(col + 1, wide), col, lax.rem(col + wide - 1, wide)]
-    halo_partners = [(side, k) for side in (0, 1, 2) for k in range(count) if (side, k) != (1, 0)]
-
-    def in_halo(side, k):
-        return {"gx": sides[side], "vert": lax.rem(me + k, count)}
+    def in_group(k):
+        return {"gx": group * group_size + lax.rem(pos + k, group_size)}
+
+    def in_joint(k):
+        return {"gx": lax.rem(group + k, groups) * group_size + pos}
+
+    def in_line(k):
+        return {"gx": lax.rem(col + k, wide)}
+
+    def send_to(k, source, slots, send_sem, recv_sem, device):
+        pltpu.make_async_remote_copy(
+            src_ref=source, dst_ref=slots.at[k - 1], send_sem=send_sem, recv_sem=recv_sem,
+            device_id=device(k), device_id_type=MESH,
+        ).start()
+
+    def all_copies(copies, slots, send_sem, recv_sem, device):
+        span = slots.at[pl.ds(0, copies)]
+        return pltpu.make_async_remote_copy(
+            src_ref=span, dst_ref=span, send_sem=send_sem, recv_sem=recv_sem,
+            device_id=device(1), device_id_type=MESH,
+        )
+
+    def slot_of(sender, mine, size):
+        return lax.rem(mine - sender - 1 + size, size)
 
     barrier = pltpu.get_barrier_semaphore()
-
-    def greet(device):
+    partners = [in_vert(k) for k in range(1, count)]
+    partners += [in_group(k) for k in range(1, group_size)]
+    partners += [in_joint(k) for k in range(1, groups)]
+    partners += [in_line(1), in_line(wide - 1)]
+    for device in partners:
         pl.semaphore_signal(barrier, inc=1, device_id=device, device_id_type=MESH)
-
-    for side, k in halo_partners:
-        greet(in_halo(side, k))
-    for k in range(1, group_size):
-        greet(in_group(lax.rem(pos + k, group_size)))
-    for k in range(1, groups):
-        greet(in_joint(lax.rem(group + k, groups)))
 
     for copy in arguments[:3]:
         copy.wait()
@@ -214,17 +224,10 @@
     mine[:, :LANES] = low
     mine[:, LANES:] = high
 
-    pl.semaphore_wait(barrier, len(halo_partners) + group_size - 1 + groups - 1)
-
-    def vert_copy(k, slot):
-        return pltpu.make_async_remote_copy(
-            src_ref=mine, dst_ref=vert_slots.at[slot],
-            send_sem=vert_send.at[k], recv_sem=vert_recv.at[slot],
-            device_id=in_vert(k), device_id_type=MESH,
-        )
+    pl.semaphore_wait(barrier, len(partners))
 
     for k in range(1, count):
-        vert_copy(k, me).start()
+        send_to(k, mine, vert_slots, vert_send, vert_recv, in_vert)
 
     for copy in arguments[3:]:
         copy.wait()
@@ -254,11 +257,10 @@
 
     lax.fori_loop(0, blocks, decays, 0)
 
-    vert_slots[me] = mine[...]
-    for k in range(1, count):
-        vert_copy(k, lax.rem(me + k, count)).wait_recv()
-    total = vert_slots[0]
-    for k in range(1, count):
+    total = mine[...]
+    vert_copies = all_copies(count - 1, vert_slots, vert_send, vert_recv, in_vert)
+    vert_copies.wait_recv()
+    for k in range(count - 1):
         total = total + vert_slots[k]
     cell = cell_values(total[:, :LANES], total[:, LANES:])
     warmth, rho = cell["warmth"], cell["rho"]
@@ -279,17 +281,10 @@
     for n, value in enumerate((rho, warmth, cell["flow_sq"], scale)):
         extra[1 + n] = value
 
-    def out_copy(p, slot):
-        return pltpu.make_async_remote_copy(
-            src_ref=message.at[p], dst_ref=arrived.at[slot],
-            send_sem=out_send.at[p], recv_sem=out_recv.at[slot],
-            device_id=in_group(p), device_id_type=MESH,
-        )
-
     def sweep(k, carry):
         p = lax.rem(pos + k, group_size)
-        for q in range(2):
-            b = 2 * p + q
+        for q in range(own):
+            b = own * p + q
             backward = lax.rem(octant_ref[b], 2)
             cx, cy, cz, wall = table[CX, b], table[CY, b], table[CZ, b], table[WALL, b]
             running = jnp.zeros((rows, LANES), F32)
@@ -306,17 +301,17 @@
                 one = att[b, s]
                 running = one * running + (1.0 - one) * source
                 gain[b, s] = running
-            message[p, q * rows : (q + 1) * rows] = running
-        message[p, 2 * rows : 2 * rows + 1] = depth_row
+            message[k - 1, q * rows : (q + 1) * rows] = running
+        message[k - 1, own * rows : own * rows + 1] = depth_row
 
         @pl.when(k < group_size)
         def _():
-            out_copy(p, pos).start()
+            send_to(k, message.at[k - 1], arrived, out_send, out_recv, in_group)
 
         return carry
 
     lax.fori_loop(1, group_size + 1, sweep, 0)
-    arrived[pos] = message[pos]
+    arrived[group_size - 1] = message[group_size - 1]
 
     def gain_sums(b, sums):
         backward = lax.rem(octant_ref[b], 2)
@@ -332,116 +327,84 @@
     for n in range(2 * columns):
         half_sums[n] = sums[n]
 
-    def wait_out(k, carry):
-        out_copy(pos, lax.rem(pos + k, group_size)).wait_recv()
-        return carry
-
-    lax.fori_loop(1, group_size, wait_out, 0)
-
+    out_copies = all_copies(group_size - 1, arrived, out_send, out_recv, in_group)
+    out_copies.wait_recv()
+
+    group_depth = zero_tile
     for j in range(group_size):
-        row = jnp.broadcast_to(arrived[j, 2 * rows : 2 * rows + 1], (rows, LANES))
+        row = jnp.broadcast_to(arrived[j, own * rows : own * rows + 1], (rows, LANES))
         depth = jnp.sum(jnp.where(diagonal, row, 0.0), axis=1, keepdims=True)
         depths[j] = jnp.broadcast_to(depth, (rows, LANES))
-    backwards = [lax.rem(octant_ref[2 * pos + q], 2) for q in range(2)]
-    for q in range(2):
-        neg_inv = table[NEG_INV, 2 * pos + q]
-        kept, running = jnp.ones((rows, LANES), F32), jnp.zeros((rows, LANES), F32)
+        group_depth = group_depth + depths[j]
+    backwards = [lax.rem(octant_ref[own * pos + q], 2) for q in range(own)]
+    for q in range(own):
+        neg_inv = table[NEG_INV, own * pos + q]
+        kept, running = jnp.ones((rows, LANES), F32), zero_tile
         for s in range(group_size):
-            t = s + backwards[q] * (group_size - 1 - 2 * s)
+            t = slot_of(s + backwards[q] * (group_size - 1 - 2 * s), pos, group_size)
             prefix[0, q, s] = kept
             prefix[1, q, s] = running
             one = jnp.exp(depths[t] * neg_inv)
             running = one * running + arrived[t, q * rows : (q + 1) * rows]
             kept = kept * one
         joint[q] = running
-        joint[2 + q] = kept
-
-    def joint_copy(g, slot):
-        return pltpu.make_async_remote_copy(
-            src_ref=joint, dst_ref=joint_slots.at[slot],
-            send_sem=joint_send.at[g], recv_sem=joint_recv.at[slot],
-            device_id=in_joint(g), device_id_type=MESH,
-        )
+    joint[own] = group_depth
 
     for k in range(1, groups):
-        joint_copy(lax.rem(group + k, groups), group).start()
-    joint_slots[group] = joint[...]
-    for k in range(1, groups):
-        joint_copy(group, lax.rem(group + k, groups)).wait_recv()
+        send_to(k, joint, joint_slots, joint_send, joint_recv, in_joint)
+    joint_slots[groups - 1] = joint[...]
+    joint_copies = all_copies(groups - 1, joint_slots, joint_send, joint_recv, in_joint)
+    joint_copies.wait_recv()
     entering = []
-    for q in range(2):
+    for q in range(own):
+        neg_inv = table[NEG_INV, own * pos + q]
         state = inflow_ref[backwards[q], :, q * LANES : (q + 1) * LANES]
         place = group + backwards[q] * (groups - 1 - 2 * group)
         for s in range(groups - 1):
-            g = s + backwards[q] * (groups - 1 - 2 * s)
+            g = slot_of(s + backwards[q] * (groups - 1 - 2 * s), group, groups)
             before = jnp.broadcast_to((place - s).astype(F32), (rows, LANES)) > 0.5
-            longer = joint_slots[g, 2 + q] * state + joint_slots[g, q]
+            longer = jnp.exp(joint_slots[g, own] * neg_inv) * state + joint_slots[g, q]
             state = jnp.where(before, longer, state)
         entering.append(state)
 
-    def back_copy(j, slot):
-        return pltpu.make_async_remote_copy(
-            src_ref=result.at[j], dst_ref=incoming.at[slot],
-            send_sem=back_send.at[j], recv_sem=back_recv.at[slot],
-            device_id=in_group(j), device_id_type=MESH,
-        )
-
-    def send_back(k, carry):
+    for k in range(1, group_size + 1):
         j = lax.rem(pos + k, group_size)
-        for q in range(2):
+        for q in range(own):
             s = j + backwards[q] * (group_size - 1 - 2 * j)
-            result[j, q] = prefix[0, q, s] * carry[q] + prefix[1, q, s]
-
-        @pl.when(k < group_size)
-        def _():
-            back_copy(j, pos).start()
-
-        return carry
-
-    lax.fori_loop(1, group_size + 1, send_back, tuple(entering))
-    incoming[pos] = result[pos]
-
-    def halves(k, sums):
-        p = lax.rem(pos + group_size - k, group_size)
-
-        @pl.when(k > 0)
-        def _():
-            back_copy(pos, p).wait_recv()
-
+            result[k - 1, q] = prefix[0, q, s] * entering[q] + prefix[1, q, s]
+        if k < group_size:
+            send_to(k, result.at[k - 1], incoming, back_send, back_recv, in_group)
+    incoming[group_size - 1] = result[group_size - 1]
+    back_copies = all_copies(group_size - 1, incoming, back_send, back_recv, in_group)
+    back_copies.wait_recv()
+
+    def entering_tile(b):
+        return incoming[slot_of(lax.div(b, own), pos, group_size), lax.rem(b, own)]
+
+    def halves(b, sums):
         sums = list(sums)
-        for q in range(2):
-            b = 2 * p + q
-            backward = lax.rem(octant_ref[b], 2)
-            weight, weight_e = table[WEIGHT, b], table[WEIGHT_E, b]
-            enter = incoming[p, q]
-            for i in range(columns):
-                s = i + backward * (columns - 1 - 2 * i)
-                value = decay[b, s] * enter
-                sums[i] = sums[i] + value * weight
-                sums[columns + i] = sums[columns + i] + value * weight_e
+        backward = lax.rem(octant_ref[b], 2)
+        weight, weight_e = table[WEIGHT, b], table[WEIGHT_E, b]
+        enter = entering_tile(b)
+        for i in range(columns):
+            value = decay[b, i + backward * (columns - 1 - 2 * i)] * enter
+            sums[i] = sums[i] + value * weight
+            sums[columns + i] = sums[columns + i] + value * weight_e
         return tuple(sums)
 
     sums = tuple(half_sums[n] for n in range(2 * columns))
-    sums = lax.fori_loop(0, group_size, halves, sums)
+    sums = lax.fori_loop(0, blocks, halves, sums)
     packed = extra[0]
     for n in range(2 * columns):
         packed = jnp.where(lane == n, jnp.sum(sums[n], axis=1, keepdims=True), packed)
     tile[...] = packed
 
-    def halo_copy(side, k, slot):
-        return pltpu.make_async_remote_copy(
-            src_ref=tile, dst_ref=halo_slots.at[side, slot],
-            send_sem=halo_send.at[side, k], recv_sem=halo_recv.at[side, slot],
-            device_id=in_halo(side, k), device_id_type=MESH,
-        )
-
-    for side, k in halo_partners:
-        halo_copy(side, k, me).start()
-    halo_slots[1, me] = tile[...]
+    for k in range(1, count):
+        send_to(k, tile, tile_slots, tile_send, tile_recv, in_vert)
 
     def form(b, carry):
         backward = lax.rem(octant_ref[b], 2)
-        enter = incoming[lax.div(b, 2), lax.rem(b, 2)]
+        enter = entering_tile(b)
         for i in range(columns):
             s = i + backward * (columns - 1 - 2 * i)
             out_ref[i, :, lane_block(b)] = decay[b, s] * enter + gain[b, s]
@@ -449,33 +412,29 @@
 
     lax.fori_loop(0, blocks, form, 0)
 
-    for k in range(1, count):
-        vert_copy(k, me).wait_send()
-    for k in range(1, groups):
-        joint_copy(lax.rem(group + k, groups), group).wait_send()
-
-    def finish_sends(k, carry):
-        p = lax.rem(pos + k, group_size)
-        out_copy(p, pos).wait_send()
-        back_copy(p, pos).wait_send()
-        return carry
-
-    lax.fori_loop(1, group_size, finish_sends, 0)
-    for side, k in halo_partners:
-        halo_copy(side, k, me).wait_send()
-
-    for side, k in halo_partners:
-        halo_copy(side, k, lax.rem(me + k, count)).wait_recv()
-    for side in range(3):
-        total = halo_slots[side, 0]
-        for k in range(1, count):
-            total = total + halo_slots[side, k]
-        total = jnp.where(lane < 2 * columns, total, halo_slots[side, 0])
-        if side == 0:
-            total = jnp.where(col == 0, 0.0, total)
-        if side == 2:
-            total = jnp.where(col == wide - 1, 0.0, total)
-        tiles_ref[side] = total
+    tile_copies = all_copies(count - 1, tile_slots, tile_send, tile_recv, in_vert)
+    tile_copies.wait_recv()
+    total = tile[...]
+    for k in range(count - 1):
+        total = total + tile_slots[k]
+    tiles_ref[1] = jnp.where(lane < 2 * columns, total, packed)
+
+    def line_copy(n, k):
+        return pltpu.make_async_remote_copy(
+            src_ref=tiles_ref.at[1], dst_ref=line_slots.at[n],
+            send_sem=line_send.at[n], recv_sem=line_recv.at[n],
+            device_id=in_line(k), device_id_type=MESH,
+        )
+
+    lines = [line_copy(0, 1), line_copy(1, wide - 1)]
+    for copy in lines:
+        copy.start()
+    for copies in (vert_copies, out_copies, joint_copies, back_copies, tile_copies):
+        copies.wait_send()
+    for copy in lines:
+        copy.wait()
+    tiles_ref[0] = jnp.where(col == 0, 0.0, line_slots[0])
+    tiles_ref[2] = jnp.where(col == wide - 1, 0.0, line_slots[1])
 
     rho, warmth, flow_sq, scale = (extra[1 + n] for n in range(4))
     change_rho, change_energy = corrections(tiles_ref)
@@ -537,9 +496,10 @@
 ):
     columns, rows, width = prior_population.shape
     blocks = width // LANES
-    group_size = blocks // 2
+    group_size = math.isqrt(wide)
+    own = blocks // group_size
     groups = wide // group_size
-    assert groups * group_size == wide and columns == 16
+    assert groups * group_size == wide and own * group_size == blocks and columns == 16
     shape = jax.ShapeDtypeStruct
     stays = pl.BlockSpec(memory_space=pltpu.HBM)
 
@@ -568,7 +528,7 @@
             pltpu.VMEM((1, width), F32),
             pltpu.VMEM((rows, columns), F32),
             pltpu.VMEM((rows, columns), jnp.int32),
-            pltpu.VMEM((2, rows, 2 * LANES), F32),
+            pltpu.VMEM((2, rows, own * LANES), F32),
             pltpu.VMEM((columns, rows, width), F32),
             tiles(7, blocks),
             tiles(MOMENTS, blocks),
@@ -585,19 +545,20 @@
             tiles(3),
             pltpu.VMEM((rows, 2 * LANES), F32),
             pltpu.VMEM((count, rows, 2 * LANES), F32),
-            pltpu.VMEM((group_size, 2 * rows + 1, LANES), F32),
-            pltpu.VMEM((group_size, 2 * rows + 1, LANES), F32),
+            pltpu.VMEM((group_size, own * rows + 1, LANES), F32),
+            pltpu.VMEM((group_size, own * rows + 1, LANES), F32),
             tiles(group_size),
-            tiles(2, 2, group_size),
-            tiles(4),
-            tiles(groups, 4),
-            tiles(group_size, 2),
-            tiles(group_size, 2),
+            tiles(2, own, group_size),
+            tiles(own + 1),
+            tiles(groups, own + 1),
+            tiles(group_size, own),
+            tiles(group_size, own),
             tiles(),
-            tiles(3, count),
-            dma(7), dma(CHUNKS), dma(count), dma(count), dma(group_size), dma(group_size),
-            dma(groups), dma(groups), dma(group_size), dma(group_size),
-            dma(3, count), dma(3, count),
+            tiles(count),
+            tiles(2),
+            dma(7), dma(CHUNKS),
+        ] + [pltpu.SemaphoreType.DMA] * 10 + [
+            dma(2), dma(2),
         ],
         compiler_params=pltpu.CompilerParams(
             collective_id=0, has_side_effects=True, vmem_limit_bytes=40 * 1024 * 1024

time: 48.6 us -> 49.4 us (1.016); the launches traced: 48.4 us -> 48.5 us
  no operation moved by 1% of the time
where the time goes in v5:
time: 49.4 us; the launch traced here: 48.5 us
  Pallas kernels  47.2 us (96%)
  local copies, waits for them, and re-layouts  1.32 us (3%)
    pallas_call x1, Pallas kernels, per_device(): pl.pallas_call(functools.partial(fused_kernel, wide, count, group_size),...  47.2 us
    unnamed x1, local copies, waits for them, and re-layouts  1.32 us

profile of v5, /device:TPU:1, one launch (start us, length us, event | category | flops | bytes accessed | tf_op | source)
XLA Modules:
  0.0 48.5 jit_solution(9557596771281024431)
XLA Ops:
  0.0 47.2 %shard_map.82 = f32[16,8,4096]{2,1,0:T(8,128)S(1)} custom-call(s32[32]{0:T(128)} %octant_in.1, f32[3,4096]{1,0:T(4,128)} %speeds_in.1, f32[1,4096]{1,0:T(1,128)} %bitcast.4, f32[1,4096]{1,0:T(1,128)} %bitcast.5, f32[8,16]{1,0:T(8,128)} %bitcast.6, s32[8,16]{1,0:T(8,128)} %bitcast.7, f32[2,8,4096]{2,1,0:T(8,128)} %inflow_in.1, f32[16,8,4096]{2,1,0:T(8,128)} %prior_in.1), custom_call_target="tpu_custom_call" | custom-call | tf_op jit(solution)/shard_map/pallas_call | solution.py:519
  47.2 1.3 %copy.10 = f32[16,8,4096]{2,1,0:T(8,128)} copy(f32[16,8,4096]{2,1,0:T(8,128)S(1)} %shard_map.82) | data formatting | bytes 4194304

commit v6 on v5

--- a/solution.py
+++ b/solution.py
@@ -83,7 +83,7 @@
     octant_in, speeds_in, jacobian_in, wall_in, collision_in, solid_in, inflow_in, prior_in,
     out_ref,
     octant_ref, speeds_ref, jacobian_ref, wall_ref, collision_ref, solid_ref, inflow_ref, prior,
-    table, moment, totals, cells, att, decay, gain, power, bell, coef, extra, half_sums, tiles_ref,
+    table, moment, cells, att, decay, gain, power, bell, coef, extra, half_sums, tiles_ref,
     mine, vert_slots, message, arrived, depths, prefix, joint, joint_slots,
     result, incoming, tile, tile_slots, line_slots,
     argument_sem, prior_sem, vert_send, vert_recv, out_send, out_recv, joint_send, joint_recv,
@@ -129,8 +129,11 @@
     def in_joint(k):
         return {"gx": lax.rem(group + k, groups) * group_size + pos}
 
-    def in_line(k):
-        return {"gx": lax.rem(col + k, wide)}
+    def in_line(side, k):
+        step = (1, 0, wide - 1)[side]
+        return {"gx": lax.rem(col + step, wide), "vert": lax.rem(me + k, count)}
+
+    lines = [(side, k) for side in (0, 2) for k in range(count)]
 
     def send_to(k, source, slots, send_sem, recv_sem, device):
         pltpu.make_async_remote_copy(
@@ -152,12 +155,14 @@
     partners = [in_vert(k) for k in range(1, count)]
     partners += [in_group(k) for k in range(1, group_size)]
     partners += [in_joint(k) for k in range(1, groups)]
-    partners += [in_line(1), in_line(wide - 1)]
+    partners += [in_line(side, k) for side, k in lines]
     for device in partners:
         pl.semaphore_signal(barrier, inc=1, device_id=device, device_id_type=MESH)
 
     for copy in arguments[:3]:
         copy.wait()
+
+    moment[...] = jnp.zeros_like(moment)
 
     def build(b, carry):
         cx, cy, cz = velocity(speeds_ref, octant_ref[b], b, rows)
@@ -179,7 +184,7 @@
             wx * square, wy * square, wz * square,
         )
         for m, entry in enumerate(entries):
-            moment[m, b] = entry
+            moment[m : m + 1, lane_block(b)] = entry[0:1]
         return carry
 
     lax.fori_loop(0, blocks, build, 0)
@@ -188,39 +193,24 @@
 
     zero_tile = jnp.zeros((rows, LANES), F32)
 
-    def pair(g, carry):
-        def add(b, sums):
-            sums = list(sums)
-            left = prior[2 * g, :, lane_block(b)]
-            right = prior[2 * g + 1, :, lane_block(b)]
-            for m in range(MOMENTS):
-                entry = moment[m, b]
-                sums[m] = sums[m] + left * entry
-                sums[MOMENTS + m] = sums[MOMENTS + m] + right * entry
-            return tuple(sums)
-
-        sums = lax.fori_loop(0, blocks, add, (zero_tile,) * (2 * MOMENTS), unroll=4)
-        for m in range(MOMENTS):
-            totals[2 * g, m] = sums[m]
-            totals[2 * g + 1, m] = sums[MOMENTS + m]
-        return carry
-
-    def moment_chunk(c, carry):
+    moment_row = lax.broadcasted_iota(jnp.int32, (16, 2 * LANES), 0)
+    place = lax.broadcasted_iota(jnp.int32, (16, 2 * LANES), 1)
+    spaced = jnp.where(place == 16 * moment_row, 1.0, 0.0)
+    for c in range(CHUNKS):
         prior_copy(c).wait()
-        return lax.fori_loop(c * (part // 2), (c + 1) * (part // 2), pair, carry)
-
-    lax.fori_loop(0, CHUNKS, moment_chunk, 0)
-
-    def pack(c, packed):
-        packed = list(packed)
-        for n in range(part):
-            for m in range(MOMENTS):
-                total = jnp.sum(totals[c * part + n, m], axis=1, keepdims=True)
-                spot = lane == (m % 8) * 16 + c * part + n
-                packed[m // 8] = jnp.where(spot, total, packed[m // 8])
-        return tuple(packed)
-
-    low, high = lax.fori_loop(0, CHUNKS, pack, (zero_tile, zero_tile))
+    field = prior[...].reshape(columns * rows, width)
+    product = lax.dot_general(
+        field, moment[...], (((1,), (1,)), ((), ())),
+        precision=lax.Precision.HIGHEST, preferred_element_type=F32,
+    )
+    product = jnp.dot(
+        product, spaced, precision=lax.Precision.HIGHEST, preferred_element_type=F32
+    )
+    low, high = product[:rows, :LANES], product[:rows, LANES:]
+    for i in range(1, columns):
+        band = product[i * rows : (i + 1) * rows]
+        low = low + pltpu.roll(band[:, :LANES], i, 1)
+        high = high + pltpu.roll(band[:, LANES:], i, 1)
     mine[:, :LANES] = low
     mine[:, LANES:] = high
 
@@ -401,6 +391,11 @@
 
     for k in range(1, count):
         send_to(k, tile, tile_slots, tile_send, tile_recv, in_vert)
+    for n, (side, k) in enumerate(lines):
+        pltpu.make_async_remote_copy(
+            src_ref=tile, dst_ref=line_slots.at[n], send_sem=line_send, recv_sem=line_recv,
+            device_id=in_line(side, k), device_id_type=MESH,
+        ).start()
 
     def form(b, carry):
         backward = lax.rem(octant_ref[b], 2)
@@ -419,22 +414,22 @@
         total = total + tile_slots[k]
     tiles_ref[1] = jnp.where(lane < 2 * columns, total, packed)
 
-    def line_copy(n, k):
-        return pltpu.make_async_remote_copy(
-            src_ref=tiles_ref.at[1], dst_ref=line_slots.at[n],
-            send_sem=line_send.at[n], recv_sem=line_recv.at[n],
-            device_id=in_line(k), device_id_type=MESH,
-        )
-
-    lines = [line_copy(0, 1), line_copy(1, wide - 1)]
-    for copy in lines:
-        copy.start()
-    for copies in (vert_copies, out_copies, joint_copies, back_copies, tile_copies):
+    def one_line(value):
+        return in_line(0, value)
+
+    line_copies = all_copies(len(lines), line_slots, line_send, line_recv, one_line)
+    line_copies.wait_recv()
+    for side, edge in ((0, 0), (2, wide - 1)):
+        slots = [line_slots[n] for n, (other, _) in enumerate(lines) if other == side]
+        total = slots[0]
+        for slot in slots[1:]:
+            total = total + slot
+        total = jnp.where(lane < 2 * columns, total, slots[0])
+        tiles_ref[side] = jnp.where(col == edge, 0.0, total)
+    for copies in (
+        vert_copies, out_copies, joint_copies, back_copies, tile_copies, line_copies
+    ):
         copies.wait_send()
-    for copy in lines:
-        copy.wait()
-    tiles_ref[0] = jnp.where(col == 0, 0.0, line_slots[0])
-    tiles_ref[2] = jnp.where(col == wide - 1, 0.0, line_slots[1])
 
     rho, warmth, flow_sq, scale = (extra[1 + n] for n in range(4))
     change_rho, change_energy = corrections(tiles_ref)
@@ -496,7 +491,7 @@
 ):
     columns, rows, width = prior_population.shape
     blocks = width // LANES
-    group_size = math.isqrt(wide)
+    group_size = min(wide, blocks // 2)
     own = blocks // group_size
     groups = wide // group_size
     assert groups * group_size == wide and own * group_size == blocks and columns == 16
@@ -531,8 +526,7 @@
             pltpu.VMEM((2, rows, own * LANES), F32),
             pltpu.VMEM((columns, rows, width), F32),
             tiles(7, blocks),
-            tiles(MOMENTS, blocks),
-            tiles(columns, MOMENTS),
+            pltpu.VMEM((16, width), F32),
             tiles(2, columns),
             tiles(blocks, columns),
             tiles(blocks, columns),
@@ -555,10 +549,9 @@
             tiles(group_size, own),
             tiles(),
             tiles(count),
-            tiles(2),
+            tiles(2 * count),
             dma(7), dma(CHUNKS),
-        ] + [pltpu.SemaphoreType.DMA] * 10 + [
-            dma(2), dma(2),
+        ] + [pltpu.SemaphoreType.DMA] * 12 + [
         ],
         compiler_params=pltpu.CompilerParams(
             collective_id=0, has_side_effects=True, vmem_limit_bytes=40 * 1024 * 1024

time: 49.4 us -> 48.1 us (0.974); the launches traced: 48.5 us -> 48 us
  Pallas kernels: 47.2 us -> 46.7 us
    pallas_call x1, Pallas kernels: 47.2 us -> 46.7 us  [per_device(): pl.pallas_call(functools.partial(fused_kernel, wide, count, group_size),...]
where the time goes in v6:
time: 48.1 us; the launch traced here: 48 us
  Pallas kernels  46.7 us (97%)
  local copies, waits for them, and re-layouts  1.32 us (3%)
    pallas_call x1, Pallas kernels, per_device(): pl.pallas_call(functools.partial(fused_kernel, wide, count, group_size),...  46.7 us
    unnamed x1, local copies, waits for them, and re-layouts  1.32 us

profile of v6, /device:TPU:1, one launch (start us, length us, event | category | flops | bytes accessed | tf_op | source)
XLA Modules:
  0.0 48.0 jit_solution(12553190002738669667)
XLA Ops:
  0.0 46.7 %shard_map.82 = f32[16,8,4096]{2,1,0:T(8,128)S(1)} custom-call(s32[32]{0:T(128)} %octant_in.1, f32[3,4096]{1,0:T(4,128)} %speeds_in.1, f32[1,4096]{1,0:T(1,128)} %bitcast.4, f32[1,4096]{1,0:T(1,128)} %bitcast.5, f32[8,16]{1,0:T(8,128)} %bitcast.6, s32[8,16]{1,0:T(8,128)} %bitcast.7, f32[2,8,4096]{2,1,0:T(8,128)} %inflow_in.1, f32[16,8,4096]{2,1,0:T(8,128)} %prior_in.1), custom_call_target="tpu_custom_call" | custom-call | tf_op jit(solution)/shard_map/pallas_call | solution.py:514
  46.7 1.3 %copy.10 = f32[16,8,4096]{2,1,0:T(8,128)} copy(f32[16,8,4096]{2,1,0:T(8,128)S(1)} %shard_map.82) | data formatting | bytes 4194304
